TPU v7x, 32 devices: a whole 2x2x4 slice. The times are simulated.
32 devices in a mesh: seq: 8 (over z, y), head: 4 (over x, core).
Axes of the slice: x: 2, y: 2, z: 4, core: 2. Of those that a mesh axis runs over, the one named last changes fastest.
Arguments:
- queries: bfloat16 [1024, 4096], P('seq', 'head'), may hold values from -6 to 6
- key_states: bfloat16 [1024, 4096], P('seq', 'head'), may hold values from -6 to 6
- value_states: bfloat16 [1024, 4096], P('seq', 'head'), may hold values from -6 to 6
- cotangent: bfloat16 [1024, 4096], P(('seq', 'head')), may hold values from -6 to 6
Outputs:
- attended: bfloat16 [1024, 4096], P(('seq', 'head'))
- query_gradient: bfloat16 [1024, 4096], P('seq', 'head')
- key_gradient: bfloat16 [1024, 4096], P('seq', 'head')
- value_gradient: bfloat16 [1024, 4096], P('seq', 'head')
All inputs are finite; a program needn't handle non-finite values.
Results may differ from a plain program's by a relative error of at most 0.011.
Values may be sent and summed in bfloat16 or wider, within the bound.
A program may use at most 64 MiB of HBM per device.

v0:
```python
import math

import jax
import jax.numpy as jnp
from jax import lax
from jax.sharding import PartitionSpec as P

HEAD_DIM = 128
LEVELS = 4


LOG_TWO = math.log(2.0)
MASKED = -1e30


def shifted(shard, axis, by):
    size = lax.axis_size(axis)
    pairs = [(i, i + by) for i in range(size) if 0 <= i + by < size]
    return lax.ppermute(shard, axis, pairs)


def pair_mean(values):
    row_count = values.shape[-2]
    grouped = values.astype(jnp.float32).reshape(
        values.shape[:-2] + (row_count // 2, 2, values.shape[-1])
    )
    return (0.5 * (grouped[..., 0, :] + grouped[..., 1, :])).astype(jnp.bfloat16)


def spread_rows(gradients):
    return jnp.repeat(0.5 * gradients, 2, axis=-2)


def span_bias(level_index, facing, block_index, blocks, block_rows):
    tier_rows = block_rows >> level_index
    distance = 2 ** (level_index - 1) + jnp.arange(block_rows // 2, dtype=jnp.int32) // tier_rows
    target = block_index + facing * distance
    valid = (target >= 0) & (target < blocks)
    return jnp.where(valid, level_index * LOG_TWO, MASKED).astype(jnp.float32)


def head_pass(query_part, key_part, value_part, key_bias, cotangent_part, score_scale):
    scores = (
        jnp.einsum("qe,ke->qk", query_part, key_part, preferred_element_type=jnp.float32)
        * score_scale
        + key_bias[None, :]
    )
    highest = jnp.max(scores, axis=1, keepdims=True)
    raised = jnp.exp(scores - highest)
    weights = raised / jnp.sum(raised, axis=1, keepdims=True)
    weights_low = weights.astype(jnp.bfloat16)
    attended = jnp.einsum(
        "qk,ke->qe", weights_low, value_part, preferred_element_type=jnp.float32
    ).astype(jnp.bfloat16)
    weight_grad = jnp.einsum(
        "qe,ke->qk", cotangent_part, value_part, preferred_element_type=jnp.float32
    )
    row_term = jnp.sum(weights * weight_grad, axis=1, keepdims=True)
    score_grad = (weights * (weight_grad - row_term) * score_scale).astype(jnp.bfloat16)
    query_grad = jnp.einsum(
        "qk,ke->qe", score_grad, key_part, preferred_element_type=jnp.float32
    ).astype(jnp.bfloat16)
    key_grad = jnp.einsum("qk,qe->ke", score_grad, query_part, preferred_element_type=jnp.float32)
    value_grad = jnp.einsum(
        "qk,qe->ke", weights_low, cotangent_part, preferred_element_type=jnp.float32
    )
    return (attended, query_grad, key_grad, value_grad)


def local(queries, key_states, value_states, cotangent):
    block_rows = queries.shape[0]
    feature_width = queries.shape[1]
    half_rows = block_rows // 2
    blocks = lax.axis_size("seq")
    block_index = lax.axis_index("seq")
    local_cotangent = lax.all_to_all(cotangent, "head", split_axis=1, concat_axis=0, tiled=True)
    stacked = jnp.stack([key_states, value_states])
    lower_spans = []
    upper_spans = []
    pyramid = [stacked]
    for level_index in range(1, LEVELS + 1):
        pyramid.append(pair_mean(pyramid[-1]))
    for level_index in range(1, LEVELS + 1):
        for facing in (-1, 1):
            pieces = []
            for distance in range(2 ** (level_index - 1), 2**level_index):
                if distance < blocks:
                    pieces.append(shifted(pyramid[level_index], "seq", -facing * distance))
                else:
                    pieces.append(jnp.zeros_like(pyramid[level_index]))
            target_list = lower_spans if facing < 0 else upper_spans
            target_list.append(jnp.concatenate(pieces, axis=1))
    key_set = jnp.concatenate([stacked] + lower_spans + upper_spans, axis=1)
    bias_parts = [jnp.zeros((block_rows,), jnp.float32)]
    for facing in (-1, 1):
        for level_index in range(1, LEVELS + 1):
            bias_parts.append(span_bias(level_index, facing, block_index, blocks, block_rows))
    key_bias = jnp.concatenate(bias_parts)
    score_scale = 1.0 / math.sqrt(HEAD_DIM)
    head_count = feature_width // HEAD_DIM
    out_columns = []
    query_columns = []
    key_columns = []
    value_columns = []
    for head_number in range(head_count):
        start_col = head_number * HEAD_DIM
        stop_col = start_col + HEAD_DIM
        results = head_pass(
            queries[:, start_col:stop_col],
            key_set[0, :, start_col:stop_col],
            key_set[1, :, start_col:stop_col],
            key_bias,
            local_cotangent[:, start_col:stop_col],
            score_scale,
        )
        out_columns.append(results[0])
        query_columns.append(results[1])
        key_columns.append(results[2])
        value_columns.append(results[3])
    local_attended = jnp.concatenate(out_columns, axis=1)
    query_gradient = jnp.concatenate(query_columns, axis=1)
    bounds = [0, block_rows] + [
        block_rows + half_rows * (number + 1) for number in range(2 * LEVELS)
    ]
    span_grads = []
    for span_number in range(2 * LEVELS + 1):
        low_row = bounds[span_number]
        high_row = bounds[span_number + 1]
        span_grads.append(
            jnp.stack(
                [
                    jnp.concatenate(
                        [grad_rows[low_row:high_row] for grad_rows in key_columns], axis=1
                    ),
                    jnp.concatenate(
                        [grad_rows[low_row:high_row] for grad_rows in value_columns], axis=1
                    ),
                ]
            )
        )
    own_grad = span_grads[0]
    lower_grads = span_grads[1 : LEVELS + 1]
    upper_grads = span_grads[LEVELS + 1 :]
    carried = None
    for level_index in range(LEVELS, 0, -1):
        tier_rows = block_rows >> level_index
        level_sum = jnp.zeros((2, tier_rows, feature_width), jnp.float32)
        for facing in (-1, 1):
            source = lower_grads if facing < 0 else upper_grads
            span_grad = source[level_index - 1]
            for distance in range(2 ** (level_index - 1), 2**level_index):
                if distance < blocks:
                    first_row = (distance - 2 ** (level_index - 1)) * tier_rows
                    part_grad = span_grad[:, first_row : first_row + tier_rows]
                    level_sum = level_sum + shifted(
                        part_grad.astype(jnp.bfloat16), "seq", facing * distance
                    ).astype(part_grad.dtype)
        carried = level_sum if carried is None else level_sum + spread_rows(carried)
    total_grad = own_grad + spread_rows(carried)
    attended = lax.all_to_all(local_attended, "head", split_axis=0, concat_axis=1, tiled=True)
    return (
        attended,
        query_gradient,
        total_grad[0].astype(jnp.bfloat16),
        total_grad[1].astype(jnp.bfloat16),
    )


def solution(mesh):
    placed = (P("seq", "head"), P("seq", "head"), P("seq", "head"), P(("seq", "head"), None))
    return jax.shard_map(
        local,
        mesh=mesh,
        in_specs=placed,
        out_specs=(P(("seq", "head"), None), P("seq", "head"), P("seq", "head"), P("seq", "head")),
        check_vma=False,
    )
```

profile of v0, /device:TPU:6, one launch (start us, length us, event | category | flops | bytes accessed | tf_op | source)
XLA Modules:
  0.0 231.0 jit_solution(153784367564203102)
XLA Ops:
  9.0 4.5 %all-to-all-start.1 = ((bf16[32,4,1024]{2,0,1:T(8,128)(2,1)}), bf16[32,4,1024]{2,0,1:T(8,128)(2,1)}, u32[]{:S(2)}, u32[]{:S(2)}) async-start(bf16[32,4,1024]{2,0,1:T(8,128)(2,1)} %bitcast.280), calls=%async_computation.1 | async-start | bytes 524288 | tf_op jit(solution)/shard_map/all_to_all | solution.py:76
  14.3 4.1 %collective-permute-start.1 = (bf16[2,32,1024]{2,0,1:T(2,128)(2,1)}, bf16[2,32,1024]{2,0,1:T(2,128)(2,1)}, u32[]{:S(2)}, u32[]{:S(2)}) collective-permute-start(bf16[2,32,1024]{2,0,1:T(2,128)(2,1)} %fusion.185), channel_id=1, source_target_pairs={{0,8},{4,12},{8,16},{12,20},{16,24},{20,28},{1,9},{5,13},{9,17},{1... | collective-permute-start | bytes 393224 | tf_op jit(solution)/shard_map/ppermute | solution.py:19
  19.2 2.8 %collective-permute-start = (bf16[2,64,1024]{2,1,0:T(8,128)(2,1)}, bf16[2,64,1024]{2,1,0:T(8,128)(2,1)S(1)}, u32[]{:S(2)}, u32[]{:S(2)}) collective-permute-start(bf16[2,64,1024]{2,1,0:T(8,128)(2,1)} %fusion.186), channel_id=1, source_target_pairs={{0,4},{4,8},{8,12},{12,16},{16,20},{20,24},{24,28},{1,5},{5,9},{9,... | collective-permute-start | bytes 786440 | tf_op jit(solution)/shard_map/ppermute | solution.py:19
  23.1 6.2 %collective-permute-done = bf16[2,64,1024]{2,1,0:T(8,128)(2,1)S(1)} collective-permute-done((bf16[2,64,1024]{2,1,0:T(8,128)(2,1)}, bf16[2,64,1024]{2,1,0:T(8,128)(2,1)S(1)}, u32[]{:S(2)}, u32[]{:S(2)}) %collective-permute-start) | collective-permute-done | bytes 262176 | tf_op jit(solution)/shard_map/ppermute | solution.py:19
  30.0 7.2 %collective-permute-start.2 = (bf16[2,32,1024]{2,0,1:T(2,128)(2,1)}, bf16[2,32,1024]{2,0,1:T(2,128)(2,1)S(1)}, u32[]{:S(2)}, u32[]{:S(2)}) collective-permute-start(bf16[2,32,1024]{2,0,1:T(2,128)(2,1)} %fusion.185), channel_id=1, source_target_pairs={{0,12},{4,16},{8,20},{12,24},{16,28},{1,13},{5,17},{9,21},{13,25},... | collective-permute-start | bytes 393224 | tf_op jit(solution)/shard_map/ppermute | solution.py:19
  38.1 1.9 collective-permute-done.2
  40.0 4.3 %collective-permute-start.3 = (bf16[2,16,1024]{2,0,1:T(2,128)(2,1)}, bf16[2,16,1024]{2,0,1:T(2,128)(2,1)S(1)}, u32[]{:S(2)}, u32[]{:S(2)}) collective-permute-start(bf16[2,16,1024]{2,0,1:T(2,128)(2,1)} %fusion.79), channel_id=1, source_target_pairs={{0,16},{4,20},{8,24},{12,28},{1,17},{5,21},{9,25},{13,29},{2,18},{... | collective-permute-start | bytes 196616 | tf_op jit(solution)/shard_map/ppermute | solution.py:19
  44.3 2.2 collective-permute-done.3
  46.5 8.9 %collective-permute-start.4 = (bf16[2,16,1024]{2,0,1:T(2,128)(2,1)}, bf16[2,16,1024]{2,0,1:T(2,128)(2,1)S(1)}, u32[]{:S(2)}, u32[]{:S(2)}) collective-permute-start(bf16[2,16,1024]{2,0,1:T(2,128)(2,1)} %fusion.79), channel_id=1, source_target_pairs={{0,20},{4,24},{8,28},{1,21},{5,25},{9,29},{2,22},{6,26},{10,30},{3... | collective-permute-start | bytes 196616 | tf_op jit(solution)/shard_map/ppermute | solution.py:19
  55.5 2.2 collective-permute-done.4
  57.6 3.8 %collective-permute-start.5 = (bf16[2,16,1024]{2,0,1:T(2,128)(2,1)}, bf16[2,16,1024]{2,0,1:T(2,128)(2,1)S(1)}, u32[]{:S(2)}, u32[]{:S(2)}) collective-permute-start(bf16[2,16,1024]{2,0,1:T(2,128)(2,1)} %fusion.79), channel_id=1, source_target_pairs={{0,24},{4,28},{1,25},{5,29},{2,26},{6,30},{3,27},{7,31}} | collective-permute-start | bytes 196616 | tf_op jit(solution)/shard_map/ppermute | solution.py:19
  61.5 2.2 collective-permute-done.5
  65.0 5.5 %collective-permute-start.7 = (bf16[2,64,1024]{2,1,0:T(8,128)(2,1)}, bf16[2,64,1024]{2,1,0:T(8,128)(2,1)S(1)}, u32[]{:S(2)}, u32[]{:S(2)}) collective-permute-start(bf16[2,64,1024]{2,1,0:T(8,128)(2,1)} %fusion.186), channel_id=1, source_target_pairs={{4,0},{8,4},{12,8},{16,12},{20,16},{24,20},{28,24},{5,1},{9,5},{13... | collective-permute-start | bytes 786440 | tf_op jit(solution)/shard_map/ppermute | solution.py:19
  70.6 7.3 %collective-permute-done.7 = bf16[2,64,1024]{2,1,0:T(8,128)(2,1)S(1)} collective-permute-done((bf16[2,64,1024]{2,1,0:T(8,128)(2,1)}, bf16[2,64,1024]{2,1,0:T(8,128)(2,1)S(1)}, u32[]{:S(2)}, u32[]{:S(2)}) %collective-permute-start.7) | collective-permute-done | bytes 262176 | tf_op jit(solution)/shard_map/ppermute | solution.py:19
  80.5 9.6 %collective-permute-done.9 = bf16[2,32,1024]{2,0,1:T(2,128)(2,1)S(1)} collective-permute-done((bf16[2,32,1024]{2,0,1:T(2,128)(2,1)}, bf16[2,32,1024]{2,0,1:T(2,128)(2,1)S(1)}, u32[]{:S(2)}, u32[]{:S(2)}) %collective-permute-start.9) | collective-permute-done | bytes 131104 | tf_op jit(solution)/shard_map/ppermute | solution.py:19
  101.7 2.5 %fusion.27 = (f32[128]{0:T(128)}, f32[128,640]{0,1:T(8,128)}) fusion(f32[128]{0:T(128)S(1)} %fusion.65, f32[640,128]{1,0:T(8,128)S(1)} %get-tuple-element.153, f32[128]{0:T(128)S(1)} %get-tuple-element.152, bf16[128,1024]{1,0:T(8,128)(2,1)} %bitcast.35, bf16[2,640,1024]{2,1,0:T(8,128)(2,1)} %copy-done), kind=kOutput, calls=%fused_computation.71 | convolution fusion | flops 21299072 | bytes 853504 | tf_op jit(solution)/shard_map/qe,ke->qk/dot_general | solution.py:55
  104.2 1.7 fusion.160
  106.1 2.3 fusion.30
  108.4 1.7 fusion.159
  110.2 2.2 fusion.33
  112.5 1.8 fusion.158
  114.4 2.2 fusion.36
  116.6 1.8 fusion.157
  118.5 2.2 fusion.39
  120.7 1.7 fusion.156
  122.5 2.3 fusion.42
  124.8 1.7 fusion.155
  128.6 1.6 fusion.153
  131.5 2.3 %fusion.45 = (f32[128]{0:T(128)}, f32[128,640]{0,1:T(8,128)}) fusion(f32[128]{0:T(128)S(1)} %fusion.53, f32[640,128]{1,0:T(8,128)S(1)} %get-tuple-element.141, f32[128]{0:T(128)S(1)} %get-tuple-element.140, bf16[128,1024]{1,0:T(8,128)(2,1)} %bitcast.35, bf16[2,640,1024]{2,1,0:T(8,128)(2,1)S(1)} %copy-done.1), kind=kOutput, calls=%fused_computation.107 | convolution fusion | flops 21299072 | bytes 853504 | tf_op jit(solution)/shard_map/qe,ke->qk/dot_general | solution.py:55
  133.8 1.7 fusion.154
  143.8 1.8 copy.93
  145.6 3.6 %all-to-all-start = ((bf16[4,32,1024]{2,1,0:T(8,128)(2,1)}), bf16[4,32,1024]{2,1,0:T(8,128)(2,1)S(1)}, u32[]{:S(2)}, u32[]{:S(2)}) async-start(bf16[4,32,1024]{2,1,0:T(8,128)(2,1)} %bitcast.32), calls=%async_computation | async-start | bytes 524288 | tf_op jit(solution)/shard_map/all_to_all | solution.py:160
  151.3 1.8 fusion.14
  154.4 1.8 fusion.13
  157.2 1.8 fusion.12
  159.3 1.8 fusion.11
  161.4 1.8 fusion.10
  163.6 1.9 fusion.9
  165.8 1.8 fusion.8
  180.0 1.3 collective-permute-start.24
  181.9 1.3 collective-permute-start.26
  185.3 1.3 collective-permute-start.18
  199.2 1.6 collective-permute-done.20
  200.7 3.2 %collective-permute-start.15 = (bf16[2,64,1024]{2,1,0:T(8,128)(2,1)S(1)}, bf16[2,64,1024]{2,1,0:T(8,128)(2,1)S(1)}, u32[]{:S(2)}, u32[]{:S(2)}) collective-permute-start(bf16[2,64,1024]{2,1,0:T(8,128)(2,1)S(1)} %pad_maximum_fusion.1), channel_id=1, source_target_pairs={{0,4},{4,8},{8,12},{12,16},{16,20},{20,24},{24,28},{1,5},{5,9},{9,... | collective-permute-start | bytes 786440 | tf_op jit(solution)/shard_map/ppermute | solution.py:19
  203.9 4.7 %collective-permute-start.14 = (bf16[2,64,1024]{2,1,0:T(8,128)(2,1)S(1)}, bf16[2,64,1024]{2,1,0:T(8,128)(2,1)}, u32[]{:S(2)}, u32[]{:S(2)}) collective-permute-start(bf16[2,64,1024]{2,1,0:T(8,128)(2,1)S(1)} %pad_maximum_fusion), channel_id=1, source_target_pairs={{4,0},{8,4},{12,8},{16,12},{20,16},{24,20},{28,24},{5,1},{9,5},{13... | collective-permute-start | bytes 786440 | tf_op jit(solution)/shard_map/ppermute | solution.py:19
  208.6 3.4 %collective-permute-start.19 = (bf16[2,32,1024]{2,1,0:T(8,128)(2,1)S(1)}, bf16[2,32,1024]{2,1,0:T(8,128)(2,1)S(1)}, u32[]{:S(2)}, u32[]{:S(2)}) collective-permute-start(bf16[2,32,1024]{2,1,0:T(8,128)(2,1)S(1)} %get-tuple-element.97), channel_id=1, source_target_pairs={{0,12},{4,16},{8,20},{12,24},{16,28},{1,13},{5,17},{9,21},{13,25},... | collective-permute-start | bytes 393224 | tf_op jit(solution)/shard_map/ppermute | solution.py:19
  215.0 5.9 %collective-permute-done.16 = bf16[2,32,1024]{2,1,0:T(8,128)(2,1)S(1)} collective-permute-done((bf16[2,32,1024]{2,1,0:T(8,128)(2,1)S(1)}, bf16[2,32,1024]{2,1,0:T(8,128)(2,1)S(1)}, u32[]{:S(2)}, u32[]{:S(2)}) %collective-permute-start.16) | collective-permute-done | bytes 131104 | tf_op jit(solution)/shard_map/ppermute | solution.py:19
  220.9 5.5 %collective-permute-done.17 = bf16[2,32,1024]{2,1,0:T(8,128)(2,1)S(1)} collective-permute-done((bf16[2,32,1024]{2,1,0:T(8,128)(2,1)S(1)}, bf16[2,32,1024]{2,1,0:T(8,128)(2,1)S(1)}, u32[]{:S(2)}, u32[]{:S(2)}) %collective-permute-start.17) | collective-permute-done | bytes 131104 | tf_op jit(solution)/shard_map/ppermute | solution.py:19
  (250 shorter events, 80.5 us)
Async XLA Ops:
  3.0 19.0 %copy-start.2 = (bf16[128,1024]{1,0:T(8,128)(2,1)S(1)}, bf16[128,1024]{1,0:T(8,128)(2,1)}, u32[]{:S(2)}) copy-start(bf16[128,1024]{1,0:T(8,128)(2,1)} %param.6) | copy-start | bytes 786436
  4.3 87.5 %collective-permute-start.13 = (bf16[2,16,1024]{2,0,1:T(2,128)(2,1)}, bf16[2,16,1024]{2,0,1:T(2,128)(2,1)}, u32[]{:S(2)}, u32[]{:S(2)}) collective-permute-start(bf16[2,16,1024]{2,0,1:T(2,128)(2,1)} %fusion.79), channel_id=1, source_target_pairs={{28,0},{29,1},{30,2},{31,3}} | collective-permute-start | bytes 196616 | tf_op jit(solution)/shard_map/ppermute | solution.py:19
  5.6 85.3 %collective-permute-start.12 = (bf16[2,16,1024]{2,0,1:T(2,128)(2,1)}, bf16[2,16,1024]{2,0,1:T(2,128)(2,1)}, u32[]{:S(2)}, u32[]{:S(2)}) collective-permute-start(bf16[2,16,1024]{2,0,1:T(2,128)(2,1)} %fusion.79), channel_id=1, source_target_pairs={{24,0},{28,4},{25,1},{29,5},{26,2},{30,6},{27,3},{31,7}} | collective-permute-start | bytes 196616 | tf_op jit(solution)/shard_map/ppermute | solution.py:19
  6.9 83.2 %collective-permute-start.11 = (bf16[2,16,1024]{2,0,1:T(2,128)(2,1)}, bf16[2,16,1024]{2,0,1:T(2,128)(2,1)}, u32[]{:S(2)}, u32[]{:S(2)}) collective-permute-start(bf16[2,16,1024]{2,0,1:T(2,128)(2,1)} %fusion.79), channel_id=1, source_target_pairs={{20,0},{24,4},{28,8},{21,1},{25,5},{29,9},{22,2},{26,6},{30,10},{2... | collective-permute-start | bytes 196616 | tf_op jit(solution)/shard_map/ppermute | solution.py:19
  9.0 92.7 %all-to-all-start.1 = ((bf16[32,4,1024]{2,0,1:T(8,128)(2,1)}), bf16[32,4,1024]{2,0,1:T(8,128)(2,1)}, u32[]{:S(2)}, u32[]{:S(2)}) async-start(bf16[32,4,1024]{2,0,1:T(8,128)(2,1)} %bitcast.280), calls=%async_computation.1 | async-start | bytes 524288 | tf_op jit(solution)/shard_map/all_to_all | solution.py:76
  14.3 15.7 %collective-permute-start.1 = (bf16[2,32,1024]{2,0,1:T(2,128)(2,1)}, bf16[2,32,1024]{2,0,1:T(2,128)(2,1)}, u32[]{:S(2)}, u32[]{:S(2)}) collective-permute-start(bf16[2,32,1024]{2,0,1:T(2,128)(2,1)} %fusion.185), channel_id=1, source_target_pairs={{0,8},{4,12},{8,16},{12,20},{16,24},{20,28},{1,9},{5,13},{9,17},{1... | collective-permute-start | bytes 393224 | tf_op jit(solution)/shard_map/ppermute | solution.py:19
  19.2 10.2 %collective-permute-start = (bf16[2,64,1024]{2,1,0:T(8,128)(2,1)}, bf16[2,64,1024]{2,1,0:T(8,128)(2,1)S(1)}, u32[]{:S(2)}, u32[]{:S(2)}) collective-permute-start(bf16[2,64,1024]{2,1,0:T(8,128)(2,1)} %fusion.186), channel_id=1, source_target_pairs={{0,4},{4,8},{8,12},{12,16},{16,20},{20,24},{24,28},{1,5},{5,9},{9,... | collective-permute-start | bytes 786440 | tf_op jit(solution)/shard_map/ppermute | solution.py:19
  23.0 71.2 %copy-start.3 = (bf16[128,1024]{1,0:T(8,128)(2,1)S(1)}, bf16[128,1024]{1,0:T(8,128)(2,1)}, u32[]{:S(2)}) copy-start(bf16[128,1024]{1,0:T(8,128)(2,1)} %param.4) | copy-start | bytes 786436
  29.3 35.6 %collective-permute-start.6 = (bf16[2,16,1024]{2,0,1:T(2,128)(2,1)}, bf16[2,16,1024]{2,0,1:T(2,128)(2,1)S(1)}, u32[]{:S(2)}, u32[]{:S(2)}) collective-permute-start(bf16[2,16,1024]{2,0,1:T(2,128)(2,1)} %fusion.79), channel_id=1, source_target_pairs={{0,28},{1,29},{2,30},{3,31}} | collective-permute-start | bytes 196616 | tf_op jit(solution)/shard_map/ppermute | solution.py:19
  30.0 10.0 %collective-permute-start.2 = (bf16[2,32,1024]{2,0,1:T(2,128)(2,1)}, bf16[2,32,1024]{2,0,1:T(2,128)(2,1)S(1)}, u32[]{:S(2)}, u32[]{:S(2)}) collective-permute-start(bf16[2,32,1024]{2,0,1:T(2,128)(2,1)} %fusion.185), channel_id=1, source_target_pairs={{0,12},{4,16},{8,20},{12,24},{16,28},{1,13},{5,17},{9,21},{13,25},... | collective-permute-start | bytes 393224 | tf_op jit(solution)/shard_map/ppermute | solution.py:19
  40.0 6.5 %collective-permute-start.3 = (bf16[2,16,1024]{2,0,1:T(2,128)(2,1)}, bf16[2,16,1024]{2,0,1:T(2,128)(2,1)S(1)}, u32[]{:S(2)}, u32[]{:S(2)}) collective-permute-start(bf16[2,16,1024]{2,0,1:T(2,128)(2,1)} %fusion.79), channel_id=1, source_target_pairs={{0,16},{4,20},{8,24},{12,28},{1,17},{5,21},{9,25},{13,29},{2,18},{... | collective-permute-start | bytes 196616 | tf_op jit(solution)/shard_map/ppermute | solution.py:19
  46.5 11.1 %collective-permute-start.4 = (bf16[2,16,1024]{2,0,1:T(2,128)(2,1)}, bf16[2,16,1024]{2,0,1:T(2,128)(2,1)S(1)}, u32[]{:S(2)}, u32[]{:S(2)}) collective-permute-start(bf16[2,16,1024]{2,0,1:T(2,128)(2,1)} %fusion.79), channel_id=1, source_target_pairs={{0,20},{4,24},{8,28},{1,21},{5,25},{9,29},{2,22},{6,26},{10,30},{3... | collective-permute-start | bytes 196616 | tf_op jit(solution)/shard_map/ppermute | solution.py:19
  57.6 6.0 %collective-permute-start.5 = (bf16[2,16,1024]{2,0,1:T(2,128)(2,1)}, bf16[2,16,1024]{2,0,1:T(2,128)(2,1)S(1)}, u32[]{:S(2)}, u32[]{:S(2)}) collective-permute-start(bf16[2,16,1024]{2,0,1:T(2,128)(2,1)} %fusion.79), channel_id=1, source_target_pairs={{0,24},{4,28},{1,25},{5,29},{2,26},{6,30},{3,27},{7,31}} | collective-permute-start | bytes 196616 | tf_op jit(solution)/shard_map/ppermute | solution.py:19
  63.6 15.5 %collective-permute-start.8 = (bf16[2,32,1024]{2,0,1:T(2,128)(2,1)}, bf16[2,32,1024]{2,0,1:T(2,128)(2,1)S(1)}, u32[]{:S(2)}, u32[]{:S(2)}) collective-permute-start(bf16[2,32,1024]{2,0,1:T(2,128)(2,1)} %fusion.185), channel_id=1, source_target_pairs={{8,0},{12,4},{16,8},{20,12},{24,16},{28,20},{9,1},{13,5},{17,9},{2... | collective-permute-start | bytes 393224 | tf_op jit(solution)/shard_map/ppermute | solution.py:19
  65.0 12.9 %collective-permute-start.7 = (bf16[2,64,1024]{2,1,0:T(8,128)(2,1)}, bf16[2,64,1024]{2,1,0:T(8,128)(2,1)S(1)}, u32[]{:S(2)}, u32[]{:S(2)}) collective-permute-start(bf16[2,64,1024]{2,1,0:T(8,128)(2,1)} %fusion.186), channel_id=1, source_target_pairs={{4,0},{8,4},{12,8},{16,12},{20,16},{24,20},{28,24},{5,1},{9,5},{13... | collective-permute-start | bytes 786440 | tf_op jit(solution)/shard_map/ppermute | solution.py:19
  77.8 12.2 %collective-permute-start.10 = (bf16[2,16,1024]{2,0,1:T(2,128)(2,1)}, bf16[2,16,1024]{2,0,1:T(2,128)(2,1)S(1)}, u32[]{:S(2)}, u32[]{:S(2)}) collective-permute-start(bf16[2,16,1024]{2,0,1:T(2,128)(2,1)} %fusion.79), channel_id=1, source_target_pairs={{16,0},{20,4},{24,8},{28,12},{17,1},{21,5},{25,9},{29,13},{18,2},{... | collective-permute-start | bytes 196616 | tf_op jit(solution)/shard_map/ppermute | solution.py:19
  79.2 10.9 %collective-permute-start.9 = (bf16[2,32,1024]{2,0,1:T(2,128)(2,1)}, bf16[2,32,1024]{2,0,1:T(2,128)(2,1)S(1)}, u32[]{:S(2)}, u32[]{:S(2)}) collective-permute-start(bf16[2,32,1024]{2,0,1:T(2,128)(2,1)} %fusion.185), channel_id=1, source_target_pairs={{12,0},{16,4},{20,8},{24,12},{28,16},{13,1},{17,5},{21,9},{25,13},... | collective-permute-start | bytes 393224 | tf_op jit(solution)/shard_map/ppermute | solution.py:19
  118.5 20.8 %copy-start.25 = (f32[128]{0:T(128)}, f32[128]{0:T(128)S(1)}, u32[]{:S(2)}) copy-start(f32[128]{0:T(128)S(1)} %fusion.57) | copy-start | bytes 1540
  122.5 15.9 %copy-start.27 = (f32[128]{0:T(128)}, f32[128]{0:T(128)S(1)}, u32[]{:S(2)}) copy-start(f32[128]{0:T(128)S(1)} %fusion.55) | copy-start | bytes 1540
  142.0 9.1 %copy-start.4 = (bf16[128,1024]{1,0:T(8,128)(2,1)S(1)}, bf16[128,1024]{1,0:T(8,128)(2,1)}, u32[]{:S(2)}) copy-start(bf16[128,1024]{1,0:T(8,128)(2,1)} %param.4) | copy-start | bytes 786436
  143.8 12.4 %copy-start.26 = (f32[128]{0:T(128)S(1)}, f32[128]{0:T(128)}, u32[]{:S(2)}) copy-start(f32[128]{0:T(128)} %copy-done.25) | copy-start | bytes 1540
  145.6 81.4 %all-to-all-start = ((bf16[4,32,1024]{2,1,0:T(8,128)(2,1)}), bf16[4,32,1024]{2,1,0:T(8,128)(2,1)S(1)}, u32[]{:S(2)}, u32[]{:S(2)}) async-start(bf16[4,32,1024]{2,1,0:T(8,128)(2,1)} %bitcast.32), calls=%async_computation | async-start | bytes 524288 | tf_op jit(solution)/shard_map/all_to_all | solution.py:160
  151.1 7.9 %copy-start.11 = (f32[128,640]{0,1:T(8,128)S(1)}, f32[128,640]{0,1:T(8,128)}, u32[]{:S(2)}) copy-start(f32[128,640]{0,1:T(8,128)} %get-tuple-element.163) | copy-start | bytes 983044
  151.1 7.8 %copy-start.32 = (f32[128]{0:T(128)S(1)}, f32[128]{0:T(128)}, u32[]{:S(2)}) copy-start(f32[128]{0:T(128)} %get-tuple-element.162) | copy-start | bytes 1540
  163.3 10.3 %copy-start.21 = (bf16[64,1024]{1,0:T(8,128)(2,1)S(1)}, bf16[64,1024]{1,0:T(8,128)(2,1)}, u32[]{:S(2)}) copy-start(bf16[64,1024]{1,0:T(8,128)(2,1)} %get-tuple-element.58) | copy-start | bytes 393220
  163.3 10.3 %copy-start.22 = (bf16[64,1024]{1,0:T(8,128)(2,1)S(1)}, bf16[64,1024]{1,0:T(8,128)(2,1)}, u32[]{:S(2)}) copy-start(bf16[64,1024]{1,0:T(8,128)(2,1)} %get-tuple-element.59) | copy-start | bytes 393220
  163.3 10.3 %copy-start.23 = (bf16[64,1024]{1,0:T(8,128)(2,1)S(1)}, bf16[64,1024]{1,0:T(8,128)(2,1)}, u32[]{:S(2)}) copy-start(bf16[64,1024]{1,0:T(8,128)(2,1)} %get-tuple-element.60) | copy-start | bytes 393220
  163.4 10.3 %copy-start.24 = (bf16[64,1024]{1,0:T(8,128)(2,1)S(1)}, bf16[64,1024]{1,0:T(8,128)(2,1)}, u32[]{:S(2)}) copy-start(bf16[64,1024]{1,0:T(8,128)(2,1)} %get-tuple-element.61) | copy-start | bytes 393220
  163.6 10.4 %copy-start.17 = (bf16[64,1024]{1,0:T(8,128)(2,1)S(1)}, bf16[64,1024]{1,0:T(8,128)(2,1)}, u32[]{:S(2)}) copy-start(bf16[64,1024]{1,0:T(8,128)(2,1)} %get-tuple-element.90) | copy-start | bytes 393220
  163.6 10.4 %copy-start.18 = (bf16[64,1024]{1,0:T(8,128)(2,1)S(1)}, bf16[64,1024]{1,0:T(8,128)(2,1)}, u32[]{:S(2)}) copy-start(bf16[64,1024]{1,0:T(8,128)(2,1)} %get-tuple-element.91) | copy-start | bytes 393220
  163.6 10.4 %copy-start.19 = (bf16[64,1024]{1,0:T(8,128)(2,1)S(1)}, bf16[64,1024]{1,0:T(8,128)(2,1)}, u32[]{:S(2)}) copy-start(bf16[64,1024]{1,0:T(8,128)(2,1)} %get-tuple-element.92) | copy-start | bytes 393220
  163.6 10.4 %copy-start.20 = (bf16[64,1024]{1,0:T(8,128)(2,1)S(1)}, bf16[64,1024]{1,0:T(8,128)(2,1)}, u32[]{:S(2)}) copy-start(bf16[64,1024]{1,0:T(8,128)(2,1)} %get-tuple-element.93) | copy-start | bytes 393220
  167.7 16.9 %copy-start.6 = (f32[128,1024]{1,0:T(8,128)}, f32[128,1024]{1,0:T(8,128)S(1)}, u32[]{:S(2)}) copy-start(f32[128,1024]{1,0:T(8,128)S(1)} %constant_dynamic-update-slice_fusion.16) | copy-start | bytes 1572868
  179.9 12.9 %copy-start.14 = (bf16[128,1024]{0,1:T(8,128)(2,1)S(1)}, bf16[128,1024]{0,1:T(8,128)(2,1)}, u32[]{:S(2)}) copy-start(bf16[128,1024]{0,1:T(8,128)(2,1)} %fusion.8) | copy-start | bytes 786436
  180.0 13.6 %collective-permute-start.24 = (bf16[2,16,1024]{2,1,0:T(8,128)(2,1)S(1)}, bf16[2,16,1024]{2,1,0:T(8,128)(2,1)S(1)}, u32[]{:S(2)}, u32[]{:S(2)}) collective-permute-start(bf16[2,16,1024]{2,1,0:T(8,128)(2,1)S(1)} %get-tuple-element.102), channel_id=1, source_target_pairs={{0,16},{4,20},{8,24},{12,28},{1,17},{5,21},{9,25},{13,29},{2,18},{... | collective-permute-start | bytes 196616 | tf_op jit(solution)/shard_map/ppermute | solution.py:19
  181.3 13.6 %collective-permute-start.27 = (bf16[2,16,1024]{2,1,0:T(8,128)(2,1)S(1)}, bf16[2,16,1024]{2,1,0:T(8,128)(2,1)S(1)}, u32[]{:S(2)}, u32[]{:S(2)}) collective-permute-start(bf16[2,16,1024]{2,1,0:T(8,128)(2,1)S(1)} %get-tuple-element.103), channel_id=1, source_target_pairs={{0,28},{1,29},{2,30},{3,31}} | collective-permute-start | bytes 196616 | tf_op jit(solution)/shard_map/ppermute | solution.py:19
  181.9 13.6 %collective-permute-start.26 = (bf16[2,16,1024]{2,1,0:T(8,128)(2,1)S(1)}, bf16[2,16,1024]{2,1,0:T(8,128)(2,1)S(1)}, u32[]{:S(2)}, u32[]{:S(2)}) collective-permute-start(bf16[2,16,1024]{2,1,0:T(8,128)(2,1)S(1)} %get-tuple-element.104), channel_id=1, source_target_pairs={{0,24},{4,28},{1,25},{5,29},{2,26},{6,30},{3,27},{7,31}} | collective-permute-start | bytes 196616 | tf_op jit(solution)/shard_map/ppermute | solution.py:19
  183.2 13.6 %collective-permute-start.25 = (bf16[2,16,1024]{2,1,0:T(8,128)(2,1)S(1)}, bf16[2,16,1024]{2,1,0:T(8,128)(2,1)S(1)}, u32[]{:S(2)}, u32[]{:S(2)}) collective-permute-start(bf16[2,16,1024]{2,1,0:T(8,128)(2,1)S(1)} %get-tuple-element.105), channel_id=1, source_target_pairs={{0,20},{4,24},{8,28},{1,21},{5,25},{9,29},{2,22},{6,26},{10,30},{3... | collective-permute-start | bytes 196616 | tf_op jit(solution)/shard_map/ppermute | solution.py:19
  185.3 28.0 %collective-permute-start.18 = (bf16[2,32,1024]{2,1,0:T(8,128)(2,1)S(1)}, bf16[2,32,1024]{2,1,0:T(8,128)(2,1)S(1)}, u32[]{:S(2)}, u32[]{:S(2)}) collective-permute-start(bf16[2,32,1024]{2,1,0:T(8,128)(2,1)S(1)} %get-tuple-element.96), channel_id=1, source_target_pairs={{0,8},{4,12},{8,16},{12,20},{16,24},{20,28},{1,9},{5,13},{9,17},{1... | collective-permute-start | bytes 393224 | tf_op jit(solution)/shard_map/ppermute | solution.py:19
  193.6 7.1 %collective-permute-start.20 = (bf16[2,16,1024]{2,1,0:T(8,128)(2,1)S(1)}, bf16[2,16,1024]{2,1,0:T(8,128)(2,1)S(1)}, u32[]{:S(2)}, u32[]{:S(2)}) collective-permute-start(bf16[2,16,1024]{2,1,0:T(8,128)(2,1)S(1)} %get-tuple-element.98), channel_id=1, source_target_pairs={{16,0},{20,4},{24,8},{28,12},{17,1},{21,5},{25,9},{29,13},{18,2},{... | collective-permute-start | bytes 196616 | tf_op jit(solution)/shard_map/ppermute | solution.py:19
  194.9 9.1 %collective-permute-start.23 = (bf16[2,16,1024]{2,1,0:T(8,128)(2,1)}, bf16[2,16,1024]{2,1,0:T(8,128)(2,1)S(1)}, u32[]{:S(2)}, u32[]{:S(2)}) collective-permute-start(bf16[2,16,1024]{2,1,0:T(8,128)(2,1)} %get-tuple-element.99), channel_id=1, source_target_pairs={{28,0},{29,1},{30,2},{31,3}} | collective-permute-start | bytes 196616 | tf_op jit(solution)/shard_map/ppermute | solution.py:19
  195.5 13.0 %collective-permute-start.22 = (bf16[2,16,1024]{2,1,0:T(8,128)(2,1)}, bf16[2,16,1024]{2,1,0:T(8,128)(2,1)S(1)}, u32[]{:S(2)}, u32[]{:S(2)}) collective-permute-start(bf16[2,16,1024]{2,1,0:T(8,128)(2,1)} %get-tuple-element.100), channel_id=1, source_target_pairs={{24,0},{28,4},{25,1},{29,5},{26,2},{30,6},{27,3},{31,7}} | collective-permute-start | bytes 196616 | tf_op jit(solution)/shard_map/ppermute | solution.py:19
  196.9 15.1 %collective-permute-start.21 = (bf16[2,16,1024]{2,1,0:T(8,128)(2,1)S(1)}, bf16[2,16,1024]{2,1,0:T(8,128)(2,1)S(1)}, u32[]{:S(2)}, u32[]{:S(2)}) collective-permute-start(bf16[2,16,1024]{2,1,0:T(8,128)(2,1)S(1)} %get-tuple-element.101), channel_id=1, source_target_pairs={{20,0},{24,4},{28,8},{21,1},{25,5},{29,9},{22,2},{26,6},{30,10},{2... | collective-permute-start | bytes 196616 | tf_op jit(solution)/shard_map/ppermute | solution.py:19
  200.7 27.0 %collective-permute-start.15 = (bf16[2,64,1024]{2,1,0:T(8,128)(2,1)S(1)}, bf16[2,64,1024]{2,1,0:T(8,128)(2,1)S(1)}, u32[]{:S(2)}, u32[]{:S(2)}) collective-permute-start(bf16[2,64,1024]{2,1,0:T(8,128)(2,1)S(1)} %pad_maximum_fusion.1), channel_id=1, source_target_pairs={{0,4},{4,8},{8,12},{12,16},{16,20},{20,24},{24,28},{1,5},{5,9},{9,... | collective-permute-start | bytes 786440 | tf_op jit(solution)/shard_map/ppermute | solution.py:19
  203.9 23.8 %collective-permute-start.14 = (bf16[2,64,1024]{2,1,0:T(8,128)(2,1)S(1)}, bf16[2,64,1024]{2,1,0:T(8,128)(2,1)}, u32[]{:S(2)}, u32[]{:S(2)}) collective-permute-start(bf16[2,64,1024]{2,1,0:T(8,128)(2,1)S(1)} %pad_maximum_fusion), channel_id=1, source_target_pairs={{4,0},{8,4},{12,8},{16,12},{20,16},{24,20},{28,24},{5,1},{9,5},{13... | collective-permute-start | bytes 786440 | tf_op jit(solution)/shard_map/ppermute | solution.py:19
  208.6 6.4 %collective-permute-start.19 = (bf16[2,32,1024]{2,1,0:T(8,128)(2,1)S(1)}, bf16[2,32,1024]{2,1,0:T(8,128)(2,1)S(1)}, u32[]{:S(2)}, u32[]{:S(2)}) collective-permute-start(bf16[2,32,1024]{2,1,0:T(8,128)(2,1)S(1)} %get-tuple-element.97), channel_id=1, source_target_pairs={{0,12},{4,16},{8,20},{12,24},{16,28},{1,13},{5,17},{9,21},{13,25},... | collective-permute-start | bytes 393224 | tf_op jit(solution)/shard_map/ppermute | solution.py:19
  212.0 8.9 %collective-permute-start.16 = (bf16[2,32,1024]{2,1,0:T(8,128)(2,1)S(1)}, bf16[2,32,1024]{2,1,0:T(8,128)(2,1)S(1)}, u32[]{:S(2)}, u32[]{:S(2)}) collective-permute-start(bf16[2,32,1024]{2,1,0:T(8,128)(2,1)S(1)} %get-tuple-element.94), channel_id=1, source_target_pairs={{8,0},{12,4},{16,8},{20,12},{24,16},{28,20},{9,1},{13,5},{17,9},{2... | collective-permute-start | bytes 393224 | tf_op jit(solution)/shard_map/ppermute | solution.py:19
  213.3 13.1 %collective-permute-start.17 = (bf16[2,32,1024]{2,1,0:T(8,128)(2,1)S(1)}, bf16[2,32,1024]{2,1,0:T(8,128)(2,1)S(1)}, u32[]{:S(2)}, u32[]{:S(2)}) collective-permute-start(bf16[2,32,1024]{2,1,0:T(8,128)(2,1)S(1)} %get-tuple-element.95), channel_id=1, source_target_pairs={{12,0},{16,4},{20,8},{24,12},{28,16},{13,1},{17,5},{21,9},{25,13},... | collective-permute-start | bytes 393224 | tf_op jit(solution)/shard_map/ppermute | solution.py:19
  (15 other events, 75.0 us)
where the time goes:
time: 235 us; the launch traced here: 231 us
  starting transfers between devices  77.2 us (33%)
  matrix products  61.7 us (26%)
  waiting for transfers between devices  44.5 us (19%)
  local copies, waits for them, and re-layouts  35.1 us (15%)
  other arithmetic  10.6 us (5%)
    ppermute x28, starting transfers between devices, shifted(): return lax.ppermute(shard, axis, pairs)  69.1 us
    ppermute x28, waiting for transfers between devices, shifted(): return lax.ppermute(shard, axis, pairs)  44.5 us
    unnamed x124, local copies, waits for them, and re-layouts  23.4 us
    dot_general x8, matrix products, head_pass(): jnp.einsum('qe,ke->qk', cotangent_part, value_part, preferred_element_typ...  17.1 us
    dot_general x8, matrix products, head_pass(): jnp.einsum('qk,qe->ke', weights_low, cotangent_part, preferred_element_ty...  13.9 us
    dot_general x8, matrix products, head_pass(): jnp.einsum('qk,ke->qe', score_grad, key_part, preferred_element_type=jnp....  13.6 us
    dot_general x8, matrix products, head_pass(): jnp.einsum('qe,ke->qk', query_part, key_part, preferred_element_type=jnp....  8.42 us
    dot_general x8, matrix products, head_pass(): jnp.einsum('qk,ke->qe', weights_low, value_part, preferred_element_type=j...  7.25 us
  transfers between devices with their start and end apart: 30, of which 10 were waited for; matrix products, arithmetic and copies ran while one was open for 24% of the time, Pallas kernels for 0%

commit v1 on v0

v1 whole, which is shorter than its diff:
```python
import functools
import math

import jax
import jax.numpy as jnp
from jax import lax
from jax.experimental import pallas as pl
from jax.experimental.pallas import tpu as pltpu
from jax.sharding import PartitionSpec as P

HEAD_DIM = 128
LEVELS = 4
GROUPS = 2

LOG_TWO = math.log(2.0)
MASKED = -1e30
MESH = pl.DeviceIdType.MESH
F32 = jnp.float32
BF16 = jnp.bfloat16


def span_slots(blocks, block_rows):
    slots = []
    start = 0
    for level in range(1, LEVELS + 1):
        rows = max(16, block_rows >> level)
        distances = [d for d in range(2 ** (level - 1), 2**level) if d < blocks]
        for facing in (-1, 1):
            for distance in distances:
                slots.append((level, facing, distance, start, rows))
                start += rows
    return slots, start


def mirror(slots, slot):
    level, facing, distance = slot[:3]
    for number, other in enumerate(slots):
        if other[:3] == (level, -facing, distance):
            return number
    return None


def contract(left, right, left_dim, right_dim):
    return lax.dot_general(
        left, right, (((left_dim,), (right_dim,)), ((), ())), preferred_element_type=F32
    )


def kernel(
    blocks, heads_axis, slots, far_rows,
    q_hbm, k_hbm, v_hbm, c_hbm,
    att_out, qg_out, kg_out, vg_out,
    keyset, q_s, cot, bias, own, gsend, grecv, att_s, pyramid,
    in_sem, cot_own_sem, att_own_sem, ksend, krecv, gsem, gland, csend, crecv, asend, arecv,
):
    block_rows, width = q_s.shape
    out_rows = c_hbm.shape[0]
    span = width // GROUPS
    me = lax.axis_index("seq")
    my_head = lax.axis_index("head")
    score_scale = 1.0 / math.sqrt(HEAD_DIM)

    def target(slot):
        other = me + slot[1] * slot[2]
        return other, (other >= 0) & (other < blocks)

    def partner(step):
        return lax.rem(my_head + step, heads_axis)

    def columns(group):
        return pl.ds(group * span, span)

    def kv_copy(group, number):
        slot = slots[number]
        other = mirror(slots, slot)
        return pltpu.make_async_remote_copy(
            src_ref=pyramid[slot[0] - 1].at[:, :, columns(group)],
            dst_ref=keyset.at[:, pl.ds(block_rows + slots[other][3], slot[4]), columns(group)],
            send_sem=ksend.at[group, number],
            recv_sem=krecv.at[group, other],
            device_id={"seq": target(slot)[0]},
            device_id_type=MESH,
        )

    def grad_copy(group, number):
        slot = slots[number]
        other = mirror(slots, slot)
        return pltpu.make_async_remote_copy(
            src_ref=gsend.at[:, pl.ds(slot[3], slot[4]), columns(group)],
            dst_ref=grecv.at[:, pl.ds(slots[other][3], slot[4]), columns(group)],
            send_sem=gsem.at[group, number],
            recv_sem=gland.at[group, other],
            device_id={"seq": target(slot)[0]},
            device_id_type=MESH,
        )

    def cot_copy(group, step):
        other = partner(step)
        return pltpu.make_async_remote_copy(
            src_ref=c_hbm.at[:, pl.ds(pl.multiple_of(other * width + group * span, 128), span)],
            dst_ref=cot.at[pl.ds(pl.multiple_of(my_head * out_rows, 16), out_rows), columns(group)],
            send_sem=csend.at[group, step - 1],
            recv_sem=crecv.at[group, step - 1],
            device_id={"head": other},
            device_id_type=MESH,
        )

    def att_copy(group, step):
        other = partner(step)
        return pltpu.make_async_remote_copy(
            src_ref=att_s.at[pl.ds(pl.multiple_of(other * out_rows, 16), out_rows), columns(group)],
            dst_ref=att_out.at[:, pl.ds(pl.multiple_of(my_head * width + group * span, 128), span)],
            send_sem=asend.at[group, step - 1],
            recv_sem=arecv.at[group, step - 1],
            device_id={"head": other},
            device_id_type=MESH,
        )

    def att_own(group):
        return pltpu.make_async_copy(
            att_s.at[pl.ds(pl.multiple_of(my_head * out_rows, 16), out_rows), columns(group)],
            att_out.at[:, pl.ds(pl.multiple_of(my_head * width + group * span, 128), span)],
            att_own_sem.at[group],
        )

    barrier = pltpu.get_barrier_semaphore()
    greeted = heads_axis - 1
    for slot in slots:
        other, valid = target(slot)
        greeted = greeted + valid.astype(jnp.int32)

        @pl.when(valid)
        def _(other=other):
            pl.semaphore_signal(barrier, inc=1, device_id={"seq": other}, device_id_type=MESH)

    for step in range(1, heads_axis):
        pl.semaphore_signal(
            barrier, inc=1, device_id={"head": partner(step)}, device_id_type=MESH
        )

    own_rows = pl.ds(0, block_rows)
    load_k = pltpu.make_async_copy(k_hbm, keyset.at[0, own_rows], in_sem.at[0])
    load_v = pltpu.make_async_copy(v_hbm, keyset.at[1, own_rows], in_sem.at[1])
    load_q = pltpu.make_async_copy(q_hbm, q_s, in_sem.at[2])
    load_c = pltpu.make_async_copy(
        c_hbm.at[:, pl.ds(pl.multiple_of(my_head * width, 128), width)],
        cot.at[pl.ds(pl.multiple_of(my_head * out_rows, 16), out_rows)],
        cot_own_sem,
    )
    load_k.start()
    load_v.start()
    load_q.start()
    load_c.start()

    for slot in slots:
        level, _, _, first, rows = slot
        other, valid = target(slot)
        row = lax.broadcasted_iota(jnp.int32, (rows, block_rows), 0)
        shown = jnp.where(valid, level * LOG_TWO, MASKED).astype(F32)
        bias[pl.ds(block_rows + first, rows), :] = jnp.where(
            row < (block_rows >> level), shown, MASKED
        )

        @pl.when(jnp.logical_not(valid))
        def _(first=first, rows=rows):
            keyset[:, pl.ds(block_rows + first, rows), :] = jnp.zeros((2, rows, width), BF16)
            grecv[:, pl.ds(first, rows), :] = jnp.zeros((2, rows, width), BF16)

    bias[own_rows, :] = jnp.zeros((block_rows, block_rows), F32)

    load_k.wait()
    load_v.wait()
    for which in range(2):
        lower = keyset[which, own_rows, :]
        for level_ref in pyramid:
            rows, wide = level_ref.shape[1], lower.shape[0]
            row = lax.broadcasted_iota(jnp.int32, (rows, wide), 0)
            col = lax.broadcasted_iota(jnp.int32, (rows, wide), 1)
            pairs = jnp.where((col >> 1) == row, 0.5, 0.0).astype(BF16)
            lower = contract(pairs, lower, 1, 0).astype(BF16)
            level_ref[which] = lower

    pl.semaphore_wait(barrier, greeted)
    for group in range(GROUPS):
        for number, slot in enumerate(slots):

            @pl.when(target(slot)[1])
            def _(group=group, number=number):
                kv_copy(group, number).start()

        for step in range(1, heads_axis):
            cot_copy(group, step).start()

    load_q.wait()
    load_c.wait()
    for group in range(GROUPS):
        for step in range(1, heads_axis):
            cot_copy(group, step).wait_recv()
        for number, slot in enumerate(slots):

            @pl.when(target(slot)[1])
            def _(group=group, number=number):
                other = mirror(slots, slots[number])
                kv_copy(group, other).wait_recv()

        def head_pass(head_number, carry, group=group):
            cols = pl.ds(pl.multiple_of(group * span + head_number * HEAD_DIM, HEAD_DIM), HEAD_DIM)
            query, key, value, grad = q_s[:, cols], keyset[0, :, cols], keyset[1, :, cols], cot[:, cols]
            scores = contract(key, query, 1, 1) * score_scale + bias[...]
            raised = jnp.exp(scores - jnp.max(scores, axis=0, keepdims=True))
            weights = raised * (1.0 / jnp.sum(raised, axis=0, keepdims=True))
            weights_low = weights.astype(BF16)
            att_s[:, cols] = contract(weights_low, value, 0, 0).astype(BF16)
            weight_grad = contract(value, grad, 1, 1)
            row_term = jnp.sum(weights * weight_grad, axis=0, keepdims=True)
            score_grad = (weights * (weight_grad - row_term) * score_scale).astype(BF16)
            qg_out[:, cols] = contract(score_grad, key, 0, 0).astype(BF16)
            for which, (left, right) in enumerate(((score_grad, query), (weights_low, grad))):
                set_grad = contract(left, right, 1, 0)
                own[which, :, cols] = set_grad[:block_rows]
                gsend[which, :, cols] = set_grad[block_rows:].astype(BF16)
            return carry

        lax.fori_loop(0, span // HEAD_DIM, head_pass, 0)
        for number, slot in enumerate(slots):

            @pl.when(target(slot)[1])
            def _(group=group, number=number):
                grad_copy(group, number).start()

        for step in range(1, heads_axis):
            att_copy(group, step).start()
        att_own(group).start()

    for group in range(GROUPS):
        for number, slot in enumerate(slots):

            @pl.when(target(slot)[1])
            def _(group=group, number=number):
                other = mirror(slots, slots[number])
                grad_copy(group, other).wait_recv()

        for which, out in enumerate((kg_out, vg_out)):
            total = own[which, :, columns(group)]
            for level in range(1, LEVELS + 1):
                spans = [slot for slot in slots if slot[0] == level]
                if not spans:
                    continue
                first, rows = spans[0][3], spans[0][4]
                count = rows * len(spans)
                row = lax.broadcasted_iota(jnp.int32, (block_rows, count), 0)
                col = lax.broadcasted_iota(jnp.int32, (block_rows, count), 1)
                spread = jnp.where(
                    (row >> level) == (col & (rows - 1)), 0.5**level, 0.0
                ).astype(BF16)
                total = total + contract(
                    spread, grecv[which, pl.ds(first, count), columns(group)], 1, 0
                )
            out[:, columns(group)] = total.astype(BF16)

    for group in range(GROUPS):
        att_own(group).wait()
        for step in range(1, heads_axis):
            cot_copy(group, step).wait_send()
            att_copy(group, step).wait()
        for number, slot in enumerate(slots):

            @pl.when(target(slot)[1])
            def _(group=group, number=number):
                kv_copy(group, number).wait_send()
                grad_copy(group, number).wait_send()


def local(blocks, heads_axis, queries, key_states, value_states, cotangent):
    block_rows, width = queries.shape
    slots, far_rows = span_slots(blocks, block_rows)
    levels = sorted({slot[0] for slot in slots})
    count = len(slots)
    steps = heads_axis - 1
    dma = pltpu.SemaphoreType.DMA
    anywhere = pl.BlockSpec(memory_space=pl.ANY)
    vmem = pl.BlockSpec(memory_space=pltpu.VMEM)
    scratch = [
        pltpu.VMEM((2, block_rows + far_rows, width), BF16),
        pltpu.VMEM((block_rows, width), BF16),
        pltpu.VMEM((block_rows, width), BF16),
        pltpu.VMEM((block_rows + far_rows, block_rows), F32),
        pltpu.VMEM((2, block_rows, width), F32),
        pltpu.VMEM((2, far_rows, width), BF16),
        pltpu.VMEM((2, far_rows, width), BF16),
        pltpu.VMEM((block_rows, width), BF16),
        [pltpu.VMEM((2, max(16, block_rows >> level), width), BF16) for level in levels],
        dma((3,)),
        dma,
        dma((GROUPS,)),
        dma((GROUPS, count)),
        dma((GROUPS, count)),
        dma((GROUPS, count)),
        dma((GROUPS, count)),
        dma((GROUPS, steps)),
        dma((GROUPS, steps)),
        dma((GROUPS, steps)),
        dma((GROUPS, steps)),
    ]
    part = jax.ShapeDtypeStruct(queries.shape, BF16)
    set_rows = block_rows + far_rows
    return pl.pallas_call(
        functools.partial(kernel, blocks, heads_axis, slots, far_rows),
        out_shape=(jax.ShapeDtypeStruct(cotangent.shape, BF16), part, part, part),
        in_specs=[anywhere] * 4,
        out_specs=(anywhere, vmem, vmem, vmem),
        scratch_shapes=scratch,
        cost_estimate=pl.CostEstimate(
            flops=12 * block_rows * set_rows * width,
            bytes_accessed=16 * block_rows * width,
            transcendentals=block_rows * set_rows * width // HEAD_DIM,
        ),
        compiler_params=pltpu.CompilerParams(
            collective_id=0, has_side_effects=True, vmem_limit_bytes=48 * 2**20
        ),
    )(queries, key_states, value_states, cotangent)


def solution(mesh):
    placed = (P("seq", "head"), P("seq", "head"), P("seq", "head"), P(("seq", "head"), None))
    return jax.shard_map(
        functools.partial(local, mesh.shape["seq"], mesh.shape["head"]),
        mesh=mesh,
        in_specs=placed,
        out_specs=(P(("seq", "head"), None), P("seq", "head"), P("seq", "head"), P("seq", "head")),
        check_vma=False,
    )
```

time: 235 us -> 55.5 us (0.24)
  the two profiles are of different devices: /device:TPU:6 before, /device:TPU:0 now
where the time goes in v1:
time: 55.5 us; the launch traced here: 55.3 us
  Pallas kernels  48 us (86%)
  local copies, waits for them, and re-layouts  6.6 us (12%)
  between operations  0.65 us (1%)
    pallas_call x1, Pallas kernels, local(): pl.pallas_call(functools.partial(kernel, blocks, heads_axis, slots, far_r...  48 us
    unnamed x12, local copies, waits for them, and re-layouts  6.6 us

profile of v1, /device:TPU:0, one launch (start us, length us, event | category | flops | bytes accessed | tf_op | source)
XLA Modules:
  0.0 55.3 jit_solution(11339370779806764398)
XLA Ops:
  0.6 0.0 copy-start
  0.6 0.9 %copy-done = bf16[128,1024]{1,0:T(8,128)(2,1)S(1)} copy-done((bf16[128,1024]{1,0:T(8,128)(2,1)S(1)}, bf16[128,1024]{1,0:T(8,128)(2,1)}, u32[]{:S(2)}) %copy-start) | copy-done | bytes 262168
  1.6 0.0 copy-start.1
  1.6 0.9 %copy-done.1 = bf16[128,1024]{1,0:T(8,128)(2,1)S(1)} copy-done((bf16[128,1024]{1,0:T(8,128)(2,1)S(1)}, bf16[128,1024]{1,0:T(8,128)(2,1)}, u32[]{:S(2)}) %copy-start.1) | copy-done | bytes 262168
  2.5 0.0 copy-start.2
  2.5 0.9 %copy-done.2 = bf16[128,1024]{1,0:T(8,128)(2,1)S(1)} copy-done((bf16[128,1024]{1,0:T(8,128)(2,1)S(1)}, bf16[128,1024]{1,0:T(8,128)(2,1)}, u32[]{:S(2)}) %copy-start.2) | copy-done | bytes 262168
  3.5 0.0 copy-start.3
  3.5 0.9 %copy-done.3 = bf16[32,4096]{1,0:T(8,128)(2,1)S(1)} copy-done((bf16[32,4096]{1,0:T(8,128)(2,1)S(1)}, bf16[32,4096]{1,0:T(8,128)(2,1)}, u32[]{:S(2)}) %copy-start.3) | copy-done | bytes 262168
  4.4 48.0 %shard_map.75 = (bf16[32,4096]{1,0:T(8,128)(2,1)S(1)}, bf16[128,1024]{1,0:T(8,128)(2,1)S(1)}, bf16[128,1024]{1,0:T(8,128)(2,1)S(1)}, bf16[128,1024]{1,0:T(8,128)(2,1)S(1)}) custom-call(bf16[128,1024]{1,0:T(8,128)(2,1)S(1)} %copy-done, bf16[128,1024]{1,0:T(8,128)(2,1)S(1)} %copy-done.1, bf16[128,1024]{1,0:T(8,128)(2,1)S(1)} %copy-done.2, ...), custom_call_target="tpu_custom_call" | custom-call | flops 805306368 | bytes 2097152 | tf_op jit(solution)/shard_map/pallas_call | solution.py:307
  52.5 0.7 %copy.12 = bf16[32,4096]{1,0:T(8,128)(2,1)} copy(bf16[32,4096]{1,0:T(8,128)(2,1)S(1)} %get-tuple-element.8) | data formatting | bytes 524288
  53.2 0.7 %copy.13 = bf16[128,1024]{1,0:T(8,128)(2,1)} copy(bf16[128,1024]{1,0:T(8,128)(2,1)S(1)} %get-tuple-element.9) | data formatting | bytes 524288
  53.9 0.7 %copy.14 = bf16[128,1024]{1,0:T(8,128)(2,1)} copy(bf16[128,1024]{1,0:T(8,128)(2,1)S(1)} %get-tuple-element.10) | data formatting | bytes 524288
  54.6 0.7 %copy.15 = bf16[128,1024]{1,0:T(8,128)(2,1)} copy(bf16[128,1024]{1,0:T(8,128)(2,1)S(1)} %get-tuple-element.11) | data formatting | bytes 524288
Async XLA Ops:
  0.6 1.0 %copy-start = (bf16[128,1024]{1,0:T(8,128)(2,1)S(1)}, bf16[128,1024]{1,0:T(8,128)(2,1)}, u32[]{:S(2)}) copy-start(bf16[128,1024]{1,0:T(8,128)(2,1)} %q_hbm.1) | copy-start | bytes 786436
  1.6 0.9 %copy-start.1 = (bf16[128,1024]{1,0:T(8,128)(2,1)S(1)}, bf16[128,1024]{1,0:T(8,128)(2,1)}, u32[]{:S(2)}) copy-start(bf16[128,1024]{1,0:T(8,128)(2,1)} %k_hbm.1) | copy-start | bytes 786436
  2.5 0.9 %copy-start.2 = (bf16[128,1024]{1,0:T(8,128)(2,1)S(1)}, bf16[128,1024]{1,0:T(8,128)(2,1)}, u32[]{:S(2)}) copy-start(bf16[128,1024]{1,0:T(8,128)(2,1)} %v_hbm.1) | copy-start | bytes 786436
  3.5 0.9 %copy-start.3 = (bf16[32,4096]{1,0:T(8,128)(2,1)S(1)}, bf16[32,4096]{1,0:T(8,128)(2,1)}, u32[]{:S(2)}) copy-start(bf16[32,4096]{1,0:T(8,128)(2,1)} %c_hbm.1) | copy-start | bytes 786436

commit v2 on v1

--- a/solution.py
+++ b/solution.py
@@ -221,7 +221,7 @@
                 gsend[which, :, cols] = set_grad[block_rows:].astype(BF16)
             return carry
 
-        lax.fori_loop(0, span // HEAD_DIM, head_pass, 0)
+        lax.fori_loop(0, span // HEAD_DIM, head_pass, 0, unroll=2)
         for number, slot in enumerate(slots):
 
             @pl.when(target(slot)[1])
@@ -269,6 +269,17 @@
             def _(group=group, number=number):
                 kv_copy(group, number).wait_send()
                 grad_copy(group, number).wait_send()
+
+
+def write_out(*refs):
+    copies = [
+        pltpu.make_async_copy(refs[number], refs[4 + number], refs[8].at[number])
+        for number in range(4)
+    ]
+    for copy in copies:
+        copy.start()
+    for copy in copies:
+        copy.wait()
 
 
 def local(blocks, heads_axis, queries, key_states, value_states, cotangent):
@@ -304,7 +315,7 @@
     ]
     part = jax.ShapeDtypeStruct(queries.shape, BF16)
     set_rows = block_rows + far_rows
-    return pl.pallas_call(
+    results = pl.pallas_call(
         functools.partial(kernel, blocks, heads_axis, slots, far_rows),
         out_shape=(jax.ShapeDtypeStruct(cotangent.shape, BF16), part, part, part),
         in_specs=[anywhere] * 4,
@@ -316,9 +327,17 @@
             transcendentals=block_rows * set_rows * width // HEAD_DIM,
         ),
         compiler_params=pltpu.CompilerParams(
-            collective_id=0, has_side_effects=True, vmem_limit_bytes=48 * 2**20
+            collective_id=0, has_side_effects=True, vmem_limit_bytes=60 * 2**20
         ),
     )(queries, key_states, value_states, cotangent)
+    return pl.pallas_call(
+        write_out,
+        out_shape=tuple(jax.ShapeDtypeStruct(part.shape, part.dtype) for part in results),
+        in_specs=[anywhere] * 4,
+        out_specs=(anywhere,) * 4,
+        scratch_shapes=[dma((4,))],
+        compiler_params=pltpu.CompilerParams(vmem_limit_bytes=60 * 2**20),
+    )(*results)
 
 
 def solution(mesh):

time: 55.5 us -> 82.6 us (1.49)
  Pallas kernels: 48 us -> 81.9 us
  local copies, waits for them, and re-layouts: 6.6 us -> 0 us
    pallas_call x0 -> x1, Pallas kernels: none -> 32.9 us  [local(): pl.pallas_call(write_out, out_shape=tuple((jax.ShapeDtypeStruct(part.shap...]
    unnamed x12 -> x0, local copies, waits for them, and re-layouts: 6.6 us -> none
    pallas_call x1, Pallas kernels: 48 us -> 49 us  [local(): pl.pallas_call(functools.partial(kernel, blocks, heads_axis, slots, far_r...]
where the time goes in v2:
time: 82.6 us; the launch traced here: 82.5 us
  Pallas kernels  81.9 us (99%)
    pallas_call x1, Pallas kernels, local(): pl.pallas_call(functools.partial(kernel, blocks, heads_axis, slots, far_r...  49 us
    pallas_call x1, Pallas kernels, local(): pl.pallas_call(write_out, out_shape=tuple((jax.ShapeDtypeStruct(part.shap...  32.9 us

profile of v2, /device:TPU:0, one launch (start us, length us, event | category | flops | bytes accessed | tf_op | source)
XLA Modules:
  0.0 82.5 jit_solution(10648678809666789353)
XLA Ops:
  0.6 49.0 %shard_map.75 = (bf16[32,4096]{1,0:T(8,128)(2,1)}, bf16[128,1024]{1,0:T(8,128)(2,1)}, bf16[128,1024]{1,0:T(8,128)(2,1)}, bf16[128,1024]{1,0:T(8,128)(2,1)}) custom-call(bf16[128,1024]{1,0:T(8,128)(2,1)} %q_hbm.1, bf16[128,1024]{1,0:T(8,128)(2,1)} %k_hbm.1, bf16[128,1024]{1,0:T(8,128)(2,1)} %v_hbm.1, bf16[32,4096]{1,0:T(8,128)(2,1)} %c_hbm.1), custom_call_target="tpu_custom_call" | custom-call | flops 805306368 | bytes 2097152 | tf_op jit(solution)/shard_map/pallas_call | solution.py:318
  49.6 32.9 %shard_map.76 = (bf16[32,4096]{1,0:T(8,128)(2,1)}, bf16[128,1024]{1,0:T(8,128)(2,1)}, bf16[128,1024]{1,0:T(8,128)(2,1)}, bf16[128,1024]{1,0:T(8,128)(2,1)}) custom-call(bf16[32,4096]{1,0:T(8,128)(2,1)} %get-tuple-element.8.refs_0_, bf16[128,1024]{1,0:T(8,128)(2,1)} %get-tuple-element.9.refs_1_, bf16[128,1024]{1,0:T(8,128)(2,1)} %get-tuple-element.10.refs_2_, ...), custom_call_target="tpu_custom_call" | custom-call | tf_op jit(solution)/shard_map/pallas_call | solution.py:333

commit v3 on v2

--- a/solution.py
+++ b/solution.py
@@ -272,14 +272,18 @@
 
 
 def write_out(*refs):
-    copies = [
-        pltpu.make_async_copy(refs[number], refs[4 + number], refs[8].at[number])
-        for number in range(4)
-    ]
-    for copy in copies:
-        copy.start()
-    for copy in copies:
-        copy.wait()
+    loads, stores = [], []
+    for number in range(4):
+        held = refs[8 + number]
+        loads.append(pltpu.make_async_copy(refs[number], held, refs[12].at[number]))
+        stores.append(pltpu.make_async_copy(held, refs[4 + number], refs[13].at[number]))
+    for load in loads:
+        load.start()
+    for load, store in zip(loads, stores):
+        load.wait()
+        store.start()
+    for store in stores:
+        store.wait()
 
 
 def local(blocks, heads_axis, queries, key_states, value_states, cotangent):
@@ -335,7 +339,7 @@
         out_shape=tuple(jax.ShapeDtypeStruct(part.shape, part.dtype) for part in results),
         in_specs=[anywhere] * 4,
         out_specs=(anywhere,) * 4,
-        scratch_shapes=[dma((4,))],
+        scratch_shapes=[pltpu.VMEM(part.shape, BF16) for part in results] + [dma((4,)), dma((4,))],
         compiler_params=pltpu.CompilerParams(vmem_limit_bytes=60 * 2**20),
     )(*results)
 

time: 82.6 us -> 51.7 us (0.63)
  Pallas kernels: 81.9 us -> 50.9 us
    pallas_call x1, Pallas kernels: 32.9 us -> 1.98 us  [local(): pl.pallas_call(write_out, out_shape=tuple((jax.ShapeDtypeStruct(part.shap...]
where the time goes in v3:
time: 51.7 us; the launch traced here: 51.6 us
  Pallas kernels  50.9 us (98%)
  between operations  0.64 us (1%)
    pallas_call x1, Pallas kernels, local(): pl.pallas_call(functools.partial(kernel, blocks, heads_axis, slots, far_r...  49 us
    pallas_call x1, Pallas kernels, local(): pl.pallas_call(write_out, out_shape=tuple((jax.ShapeDtypeStruct(part.shap...  1.98 us

profile of v3, /device:TPU:0, one launch (start us, length us, event | category | flops | bytes accessed | tf_op | source)
XLA Modules:
  0.0 51.6 jit_solution(17832821523578758514)
XLA Ops:
  0.6 49.0 %shard_map.75 = (bf16[32,4096]{1,0:T(8,128)(2,1)}, bf16[128,1024]{1,0:T(8,128)(2,1)}, bf16[128,1024]{1,0:T(8,128)(2,1)}, bf16[128,1024]{1,0:T(8,128)(2,1)}) custom-call(bf16[128,1024]{1,0:T(8,128)(2,1)} %q_hbm.1, bf16[128,1024]{1,0:T(8,128)(2,1)} %k_hbm.1, bf16[128,1024]{1,0:T(8,128)(2,1)} %v_hbm.1, bf16[32,4096]{1,0:T(8,128)(2,1)} %c_hbm.1), custom_call_target="tpu_custom_call" | custom-call | flops 805306368 | bytes 2097152 | tf_op jit(solution)/shard_map/pallas_call | solution.py:322
  49.6 2.0 %shard_map.76 = (bf16[32,4096]{1,0:T(8,128)(2,1)}, bf16[128,1024]{1,0:T(8,128)(2,1)}, bf16[128,1024]{1,0:T(8,128)(2,1)}, bf16[128,1024]{1,0:T(8,128)(2,1)}) custom-call(bf16[32,4096]{1,0:T(8,128)(2,1)} %get-tuple-element.8.refs_0_, bf16[128,1024]{1,0:T(8,128)(2,1)} %get-tuple-element.9.refs_1_, bf16[128,1024]{1,0:T(8,128)(2,1)} %get-tuple-element.10.refs_2_, ...), custom_call_target="tpu_custom_call" | custom-call | tf_op jit(solution)/shard_map/pallas_call | solution.py:337

commit v4 on v3

v4 whole, which is shorter than its diff:
```python
import functools
import math

import jax
import jax.numpy as jnp
from jax import lax
from jax.experimental import pallas as pl
from jax.experimental.pallas import tpu as pltpu
from jax.sharding import PartitionSpec as P

HEAD_DIM = 128
LEVELS = 4
GROUPS = 2

LOG_TWO = math.log(2.0)
MASKED = -1e30
MESH = pl.DeviceIdType.MESH
F32 = jnp.float32
BF16 = jnp.bfloat16


def rows_of(level, block_rows):
    return max(16, block_rows >> level)


class Plan:
    def __init__(self, blocks, block_rows):
        self.pairs = blocks // 2
        farthest = 2**LEVELS - 1
        self.reach = min((farthest + 1) // 2, self.pairs - 1)
        self.entries = []
        self.first = []
        self.uses = [[], []]
        self.far_rows = [0, 0]
        self.returns = [[], []]
        self.return_rows = [0, 0]
        self.entry_rows = 0
        for t in range(2):
            self.use(t, None, 1, block_rows)
        for distance in range(1, self.reach + 1):
            for offset in (distance, -distance):
                for part in range(2):
                    gaps = [abs(2 * offset + part - t) for t in range(2)]
                    levels = [gap.bit_length() if gap <= farthest else None for gap in gaps]
                    known = [level for level in levels if level is not None]
                    if not known:
                        continue
                    level = min(known)
                    rows = rows_of(level, block_rows)
                    number = len(self.entries)
                    self.entries.append((offset, part, level, rows))
                    self.first.append(self.entry_rows)
                    self.entry_rows += rows
                    self.returns[part].append((number, self.return_rows[part]))
                    self.return_rows[part] += rows
                    for t in range(2):
                        if levels[t] is not None:
                            self.use(t, number, levels[t], block_rows)

    def use(self, t, number, level, block_rows):
        rows = rows_of(level, block_rows)
        self.uses[t].append((number, level, self.far_rows[t], rows))
        self.far_rows[t] += rows

    def return_first(self, number):
        part = self.entries[number][1]
        return dict(self.returns[part])[number]


def contract(left, right, left_dim, right_dim):
    return lax.dot_general(
        left, right, (((left_dim,), (right_dim,)), ((), ())), preferred_element_type=F32
    )


def pair_matrix(rows, wide):
    row = lax.broadcasted_iota(jnp.int32, (rows, wide), 0)
    col = lax.broadcasted_iota(jnp.int32, (rows, wide), 1)
    return jnp.where((col >> 1) == row, 0.5, 0.0).astype(BF16)


def kernel(
    plan, heads_axis,
    q_hbm, k_hbm, v_hbm, c_hbm,
    att_out, qg_out, kg_out, vg_out,
    keyset, q_s, cot, bias, own, far_grad, rbuf, gsend, grecv, spread, att_s, qg_s, total_s, pyramid,
    own_sem, cot_own_sem, out_own_sem, att_own_sem, send_in, recv_in, ksend, krecv,
    gsem, gland, csend, crecv, asend, arecv, send_out, recv_out,
):
    block_rows, width = q_hbm.shape
    out_rows = c_hbm.shape[0]
    half = width // 2
    span = half // GROUPS
    entries = plan.entries
    position = lax.axis_index("seq")
    my_head = lax.axis_index("head")
    pair, mine = position // 2, position % 2
    mate = 2 * pair + 1 - mine
    crew = 2 * heads_axis
    my_seat = mine * heads_axis + my_head
    own_rows = pl.ds(0, block_rows)
    score_scale = 1.0 / math.sqrt(HEAD_DIM)

    def inside(other):
        return (other >= 0) & (other < plan.pairs)

    def rail(other):
        return {"seq": 2 * other + mine, "head": my_head}

    def seat(step):
        other = (my_seat + step) % crew
        return other // heads_axis, other % heads_axis

    def columns(group):
        return pl.ds(group * span, span)

    def side(part, group):
        return pl.ds(pl.multiple_of(part * half + group * span, 128), span)

    def remote(src, dst, send_sem, recv_sem, device):
        return pltpu.make_async_remote_copy(
            src_ref=src, dst_ref=dst, send_sem=send_sem, recv_sem=recv_sem,
            device_id=device, device_id_type=MESH,
        )

    def block_place(which, part, group):
        if which == 2:
            return q_s.at[part, :, columns(group)]
        return keyset.at[part, which, own_rows, columns(group)]

    def own_copy(which, group):
        return pltpu.make_async_copy(
            (k_hbm, v_hbm, q_hbm)[which].at[:, side(mine, group)],
            block_place(which, mine, group),
            own_sem.at[which, group],
        )

    def mate_copy(which, group):
        return remote(
            (k_hbm, v_hbm, q_hbm)[which].at[:, side(1 - mine, group)],
            block_place(which, mine, group),
            send_in.at[which, group],
            recv_in.at[which, group],
            {"seq": mate, "head": my_head},
        )

    def cot_source(part, other_head, group):
        first = other_head * width + part * half + group * span
        return c_hbm.at[:, pl.ds(pl.multiple_of(first, 128), span)]

    def cot_place(group):
        return cot.at[mine, pl.ds(pl.multiple_of(my_head * out_rows, 16), out_rows), columns(group)]

    def cot_copy(group, step):
        part, other = seat(step)
        return remote(
            cot_source(part, other, group), cot_place(group),
            csend.at[group, step - 1], crecv.at[group, step - 1],
            {"seq": 2 * pair + part, "head": other},
        )

    def cot_own(group):
        return pltpu.make_async_copy(
            cot_source(mine, my_head, group), cot_place(group), cot_own_sem.at[group]
        )

    def att_source(part, other_head, group):
        return att_s.at[
            part, pl.ds(pl.multiple_of(other_head * out_rows, 16), out_rows), columns(group)
        ]

    def att_place(group):
        first = my_head * width + mine * half + group * span
        return att_out.at[:, pl.ds(pl.multiple_of(first, 128), span)]

    def att_copy(group, step):
        part, other = seat(step)
        return remote(
            att_source(part, other, group), att_place(group),
            asend.at[group, step - 1], arecv.at[group, step - 1],
            {"seq": 2 * pair + part, "head": other},
        )

    def att_own(group):
        return pltpu.make_async_copy(
            att_source(mine, my_head, group), att_place(group), att_own_sem.at[group]
        )

    def kv_copy(group, number):
        offset, part, level, rows = entries[number]
        return remote(
            pyramid[level - 1].at[part, :, :, columns(group)],
            rbuf.at[:, pl.ds(plan.first[number], rows), columns(group)],
            ksend.at[group, number], krecv.at[group, number], rail(pair - offset),
        )

    def grad_copy(group, number):
        offset, part, level, rows = entries[number]
        return remote(
            gsend.at[:, pl.ds(plan.first[number], rows), columns(group)],
            grecv.at[part, :, pl.ds(plan.return_first(number), rows), columns(group)],
            gsem.at[group, number], gland.at[group, number], rail(pair + offset),
        )

    def result(which, part, group):
        if which == 0:
            return qg_s.at[part, :, columns(group)]
        return total_s.at[part, which - 1, :, columns(group)]

    def result_own(which, group):
        return pltpu.make_async_copy(
            result(which, mine, group),
            (qg_out, kg_out, vg_out)[which].at[:, side(mine, group)],
            out_own_sem.at[which, group],
        )

    def result_copy(which, group):
        return remote(
            result(which, 1 - mine, group),
            (qg_out, kg_out, vg_out)[which].at[:, side(mine, group)],
            send_out.at[which, group], recv_out.at[which, group],
            {"seq": mate, "head": my_head},
        )

    def make_levels(part, group):
        for which in range(2):
            lower = keyset[part, which, own_rows, columns(group)]
            for level_ref in pyramid:
                pairs = pair_matrix(level_ref.shape[2], lower.shape[0])
                lower = contract(pairs, lower, 1, 0).astype(BF16)
                level_ref[part, which, :, columns(group)] = lower

    def send_levels(part, group):
        for number, entry in enumerate(entries):
            if entry[1] == part:

                @pl.when(inside(pair - entry[0]))
                def _(number=number):
                    kv_copy(group, number).start()

    barrier = pltpu.get_barrier_semaphore()
    greeted = crew - 1
    for step in range(1, crew):
        part, other = seat(step)
        pl.semaphore_signal(
            barrier, inc=1,
            device_id={"seq": 2 * pair + part, "head": other}, device_id_type=MESH,
        )
    for distance in range(1, plan.reach + 1):
        for offset in (distance, -distance):
            valid = inside(pair + offset)
            greeted = greeted + valid.astype(jnp.int32)

            @pl.when(valid)
            def _(offset=offset):
                pl.semaphore_signal(
                    barrier, inc=1, device_id=rail(pair + offset), device_id_type=MESH
                )

    for which in range(3):
        for group in range(GROUPS):
            own_copy(which, group).start()
    for group in range(GROUPS):
        cot_own(group).start()

    pl.semaphore_wait(barrier, greeted)
    for group in range(GROUPS):
        for which in range(2):
            mate_copy(which, group).start()

    for group in range(GROUPS):
        for which in range(2):
            own_copy(which, group).wait()
        for part in range(2):

            @pl.when(mine == part)
            def _(part=part, group=group):
                make_levels(part, group)
                send_levels(part, group)

    for group in range(GROUPS):
        for which in range(2):
            mate_copy(which, group).wait_recv()
        for part in range(2):

            @pl.when(mine != part)
            def _(part=part, group=group):
                make_levels(part, group)
                send_levels(part, group)

        mate_copy(2, group).start()
        for step in range(1, crew):
            cot_copy(group, step).start()

    for t in range(2):
        bias[t, own_rows, :] = jnp.zeros((block_rows, block_rows), F32)
        for number, level, first, rows in plan.uses[t]:
            row = lax.broadcasted_iota(jnp.int32, (rows, block_rows), 0)
            shown = level * LOG_TWO
            if number is not None:
                valid = inside(pair + entries[number][0])
                shown = jnp.where(valid, shown, MASKED).astype(F32)

                @pl.when(jnp.logical_not(valid))
                def _(t=t, first=first, rows=rows):
                    keyset[t, :, pl.ds(block_rows + first, rows), :] = jnp.zeros(
                        (2, rows, half), BF16
                    )

            bias[t, pl.ds(block_rows + first, rows), :] = jnp.where(
                row < (block_rows >> level), shown, MASKED
            )
        for number, first in plan.returns[t]:
            offset, _, level, rows = entries[number]
            row = lax.broadcasted_iota(jnp.int32, (rows, block_rows), 0)
            col = lax.broadcasted_iota(jnp.int32, (rows, block_rows), 1)
            spread[t, pl.ds(first, rows), :] = jnp.where(
                (col >> level) == row, 0.5**level, 0.0
            ).astype(BF16)

            @pl.when(jnp.logical_not(inside(pair - offset)))
            def _(t=t, first=first, rows=rows):
                grecv[t, :, pl.ds(first, rows), :] = jnp.zeros((2, rows, half), BF16)

    for group in range(GROUPS):
        own_copy(2, group).wait()
        cot_own(group).wait()
        mate_copy(2, group).wait_recv()
        for step in range(1, crew):
            cot_copy(group, step).wait_recv()
        for t in range(2):
            _, _, first, rows = plan.uses[t][0]
            keyset[t, :, pl.ds(block_rows + first, rows), columns(group)] = pyramid[0][
                1 - t, :, :, columns(group)
            ]
        for number, (offset, _, level, rows) in enumerate(entries):

            @pl.when(inside(pair + offset))
            def _(group=group, number=number, level=level, rows=rows):
                kv_copy(group, number).wait_recv()
                for which in range(2):
                    fine = rbuf[which, pl.ds(plan.first[number], rows), columns(group)]
                    for t in range(2):
                        for other, use_level, first, use_rows in plan.uses[t]:
                            if other == number:
                                held = fine
                                if use_level != level:
                                    held = contract(pair_matrix(use_rows, rows), fine, 1, 0)
                                keyset[
                                    t, which, pl.ds(block_rows + first, use_rows), columns(group)
                                ] = held.astype(BF16)

        def head_pass(head_number, carry, group=group):
            cols = pl.ds(pl.multiple_of(group * span + head_number * HEAD_DIM, HEAD_DIM), HEAD_DIM)
            for t in range(2):
                set_rows = pl.ds(0, block_rows + plan.far_rows[t])
                query, grad = q_s[t, :, cols], cot[t, :, cols]
                key, value = keyset[t, 0, set_rows, cols], keyset[t, 1, set_rows, cols]
                scores = contract(key, query, 1, 1) * score_scale + bias[t, set_rows, :]
                raised = jnp.exp(scores - jnp.max(scores, axis=0, keepdims=True))
                weights = raised * (1.0 / jnp.sum(raised, axis=0, keepdims=True))
                weights_low = weights.astype(BF16)
                att_s[t, :, cols] = contract(weights_low, value, 0, 0).astype(BF16)
                weight_grad = contract(value, grad, 1, 1)
                row_term = jnp.sum(weights * weight_grad, axis=0, keepdims=True)
                score_grad = (weights * (weight_grad - row_term) * score_scale).astype(BF16)
                qg_s[t, :, cols] = contract(score_grad, key, 0, 0).astype(BF16)
                for which, (left, right) in enumerate(((score_grad, query), (weights_low, grad))):
                    set_grad = contract(left, right, 1, 0)
                    own[t, which, :, cols] = set_grad[:block_rows]
                    far_grad[t, which, pl.ds(0, plan.far_rows[t]), cols] = set_grad[
                        block_rows:
                    ].astype(BF16)
            return carry

        lax.fori_loop(0, span // HEAD_DIM, head_pass, 0)
        for number, (offset, _, level, rows) in enumerate(entries):

            @pl.when(inside(pair + offset))
            def _(group=group, number=number, level=level, rows=rows):
                for which in range(2):
                    summed = None
                    for t in range(2):
                        for other, use_level, first, use_rows in plan.uses[t]:
                            if other == number:
                                term = far_grad[t, which, pl.ds(first, use_rows), columns(group)]
                                if use_level != level:
                                    term = contract(pair_matrix(use_rows, rows), term, 0, 0)
                                term = term.astype(F32)
                                summed = term if summed is None else summed + term
                    gsend[which, pl.ds(plan.first[number], rows), columns(group)] = summed.astype(
                        BF16
                    )
                grad_copy(group, number).start()

        for step in range(1, crew):
            att_copy(group, step).start()
        att_own(group).start()
        result_copy(0, group).start()
        result_own(0, group).start()

    for group in range(GROUPS):
        for number, (offset, _, _, _) in enumerate(entries):

            @pl.when(inside(pair - offset))
            def _(group=group, number=number):
                grad_copy(group, number).wait_recv()

        for u in range(2):
            _, _, first, rows = plan.uses[1 - u][0]
            near = pair_matrix(rows, block_rows)
            returned = pl.ds(0, plan.return_rows[u])
            for which in range(2):
                total = own[u, which, :, columns(group)]
                total = total + contract(
                    near, far_grad[1 - u, which, pl.ds(first, rows), columns(group)], 0, 0
                )
                total = total + contract(
                    spread[u, returned, :], grecv[u, which, returned, columns(group)], 0, 0
                )
                total_s[u, which, :, columns(group)] = total.astype(BF16)
        for which in (1, 2):
            result_copy(which, group).start()
            result_own(which, group).start()

    for group in range(GROUPS):
        att_own(group).wait()
        for which in range(3):
            result_own(which, group).wait()
            result_copy(which, group).wait()
            mate_copy(which, group).wait_send()
        for step in range(1, crew):
            cot_copy(group, step).wait_send()
            att_copy(group, step).wait()
        for number, (offset, _, _, _) in enumerate(entries):

            @pl.when(inside(pair - offset))
            def _(group=group, number=number):
                kv_copy(group, number).wait_send()

            @pl.when(inside(pair + offset))
            def _(group=group, number=number):
                grad_copy(group, number).wait_send()


def write_out(*refs):
    loads, stores = [], []
    for number in range(4):
        held = refs[8 + number]
        loads.append(pltpu.make_async_copy(refs[number], held, refs[12].at[number]))
        stores.append(pltpu.make_async_copy(held, refs[4 + number], refs[13].at[number]))
    for load in loads:
        load.start()
    for load, store in zip(loads, stores):
        load.wait()
        store.start()
    for store in stores:
        store.wait()


def local(blocks, heads_axis, queries, key_states, value_states, cotangent):
    block_rows, width = queries.shape
    plan = Plan(blocks, block_rows)
    half = width // 2
    count = len(plan.entries)
    far_rows, return_rows = max(plan.far_rows), max(plan.return_rows)
    set_rows = block_rows + far_rows
    levels = max(entry[2] for entry in plan.entries)
    steps = 2 * heads_axis - 1
    dma = pltpu.SemaphoreType.DMA
    anywhere = pl.BlockSpec(memory_space=pl.ANY)
    scratch = [
        pltpu.VMEM((2, 2, set_rows, half), BF16),
        pltpu.VMEM((2, block_rows, half), BF16),
        pltpu.VMEM((2, block_rows, half), BF16),
        pltpu.VMEM((2, set_rows, block_rows), F32),
        pltpu.VMEM((2, 2, block_rows, half), F32),
        pltpu.VMEM((2, 2, far_rows, half), BF16),
        pltpu.VMEM((2, plan.entry_rows, half), BF16),
        pltpu.VMEM((2, plan.entry_rows, half), BF16),
        pltpu.VMEM((2, 2, return_rows, half), BF16),
        pltpu.VMEM((2, return_rows, block_rows), BF16),
        pltpu.VMEM((2, block_rows, half), BF16),
        pltpu.VMEM((2, block_rows, half), BF16),
        pltpu.VMEM((2, 2, block_rows, half), BF16),
        [
            pltpu.VMEM((2, 2, rows_of(level, block_rows), half), BF16)
            for level in range(1, levels + 1)
        ],
        dma((3, GROUPS)),
        dma((GROUPS,)),
        dma((3, GROUPS)),
        dma((GROUPS,)),
        dma((3, GROUPS)),
        dma((3, GROUPS)),
        dma((GROUPS, count)),
        dma((GROUPS, count)),
        dma((GROUPS, count)),
        dma((GROUPS, count)),
        dma((GROUPS, steps)),
        dma((GROUPS, steps)),
        dma((GROUPS, steps)),
        dma((GROUPS, steps)),
        dma((3, GROUPS)),
        dma((3, GROUPS)),
    ]
    part = jax.ShapeDtypeStruct(queries.shape, BF16)
    results = pl.pallas_call(
        functools.partial(kernel, plan, heads_axis),
        out_shape=(jax.ShapeDtypeStruct(cotangent.shape, BF16), part, part, part),
        in_specs=[anywhere] * 4,
        out_specs=(anywhere,) * 4,
        scratch_shapes=scratch,
        cost_estimate=pl.CostEstimate(
            flops=12 * block_rows * set_rows * width,
            bytes_accessed=16 * block_rows * width,
            transcendentals=block_rows * set_rows * width // HEAD_DIM,
        ),
        compiler_params=pltpu.CompilerParams(
            collective_id=0, has_side_effects=True, vmem_limit_bytes=60 * 2**20
        ),
    )(queries, key_states, value_states, cotangent)
    return pl.pallas_call(
        write_out,
        out_shape=tuple(jax.ShapeDtypeStruct(part.shape, part.dtype) for part in results),
        in_specs=[anywhere] * 4,
        out_specs=(anywhere,) * 4,
        scratch_shapes=[pltpu.VMEM(part.shape, BF16) for part in results] + [dma((4,)), dma((4,))],
        compiler_params=pltpu.CompilerParams(vmem_limit_bytes=60 * 2**20),
    )(*results)


def solution(mesh):
    placed = (P("seq", "head"), P("seq", "head"), P("seq", "head"), P(("seq", "head"), None))
    return jax.shard_map(
        functools.partial(local, mesh.shape["seq"], mesh.shape["head"]),
        mesh=mesh,
        in_specs=placed,
        out_specs=(P(("seq", "head"), None), P("seq", "head"), P("seq", "head"), P("seq", "head")),
        check_vma=False,
    )
```

time: 51.7 us -> 42.9 us (0.83)
  Pallas kernels: 50.9 us -> 42.1 us
    pallas_call x1, Pallas kernels: 49 us -> 40.1 us  [local(): pl.pallas_call(functools.partial(kernel, plan, heads_axis), out_shape=(ja...]
where the time goes in v4:
time: 42.9 us; the launch traced here: 42.7 us
  Pallas kernels  42.1 us (98%)
  between operations  0.64 us (1%)
    pallas_call x1, Pallas kernels, local(): pl.pallas_call(functools.partial(kernel, plan, heads_axis), out_shape=(ja...  40.1 us
    pallas_call x1, Pallas kernels, local(): pl.pallas_call(write_out, out_shape=tuple((jax.ShapeDtypeStruct(part.shap...  1.98 us

profile of v4, /device:TPU:0, one launch (start us, length us, event | category | flops | bytes accessed | tf_op | source)
XLA Modules:
  0.0 42.7 jit_solution(12749233844598418953)
XLA Ops:
  0.6 40.1 %shard_map.75 = (bf16[32,4096]{1,0:T(8,128)(2,1)}, bf16[128,1024]{1,0:T(8,128)(2,1)}, bf16[128,1024]{1,0:T(8,128)(2,1)}, bf16[128,1024]{1,0:T(8,128)(2,1)}) custom-call(bf16[128,1024]{1,0:T(8,128)(2,1)} %q_hbm.1, bf16[128,1024]{1,0:T(8,128)(2,1)} %k_hbm.1, bf16[128,1024]{1,0:T(8,128)(2,1)} %v_hbm.1, bf16[32,4096]{1,0:T(8,128)(2,1)} %c_hbm.1), custom_call_target="tpu_custom_call" | custom-call | flops 780140544 | bytes 2097152 | tf_op jit(solution)/shard_map/pallas_call | solution.py:508
  40.8 2.0 %shard_map.76 = (bf16[32,4096]{1,0:T(8,128)(2,1)}, bf16[128,1024]{1,0:T(8,128)(2,1)}, bf16[128,1024]{1,0:T(8,128)(2,1)}, bf16[128,1024]{1,0:T(8,128)(2,1)}) custom-call(bf16[32,4096]{1,0:T(8,128)(2,1)} %get-tuple-element.8.refs_0_, bf16[128,1024]{1,0:T(8,128)(2,1)} %get-tuple-element.9.refs_1_, bf16[128,1024]{1,0:T(8,128)(2,1)} %get-tuple-element.10.refs_2_, ...), custom_call_target="tpu_custom_call" | custom-call | tf_op jit(solution)/shard_map/pallas_call | solution.py:523

commit v5 on v4

--- a/solution.py
+++ b/solution.py
@@ -10,7 +10,7 @@
 
 HEAD_DIM = 128
 LEVELS = 4
-GROUPS = 2
+GROUPS = 4
 
 LOG_TWO = math.log(2.0)
 MASKED = -1e30
@@ -238,6 +238,30 @@
                 def _(number=number):
                     kv_copy(group, number).start()
 
+    def finish(group):
+        for number, (offset, _, _, _) in enumerate(entries):
+
+            @pl.when(inside(pair - offset))
+            def _(group=group, number=number):
+                grad_copy(group, number).wait_recv()
+
+        for u in range(2):
+            _, _, first, rows = plan.uses[1 - u][0]
+            near = pair_matrix(rows, block_rows)
+            returned = pl.ds(0, plan.return_rows[u])
+            for which in range(2):
+                total = own[u, which, :, columns(group)]
+                total = total + contract(
+                    near, far_grad[1 - u, which, pl.ds(first, rows), columns(group)], 0, 0
+                )
+                total = total + contract(
+                    spread[u, returned, :], grecv[u, which, returned, columns(group)], 0, 0
+                )
+                total_s[u, which, :, columns(group)] = total.astype(BF16)
+        for which in (1, 2):
+            result_copy(which, group).start()
+            result_own(which, group).start()
+
     barrier = pltpu.get_barrier_semaphore()
     greeted = crew - 1
     for step in range(1, crew):
@@ -296,7 +320,7 @@
         bias[t, own_rows, :] = jnp.zeros((block_rows, block_rows), F32)
         for number, level, first, rows in plan.uses[t]:
             row = lax.broadcasted_iota(jnp.int32, (rows, block_rows), 0)
-            shown = level * LOG_TWO
+            shown = float(level)
             if number is not None:
                 valid = inside(pair + entries[number][0])
                 shown = jnp.where(valid, shown, MASKED).astype(F32)
@@ -352,20 +376,32 @@
 
         def head_pass(head_number, carry, group=group):
             cols = pl.ds(pl.multiple_of(group * span + head_number * HEAD_DIM, HEAD_DIM), HEAD_DIM)
-            for t in range(2):
-                set_rows = pl.ds(0, block_rows + plan.far_rows[t])
-                query, grad = q_s[t, :, cols], cot[t, :, cols]
-                key, value = keyset[t, 0, set_rows, cols], keyset[t, 1, set_rows, cols]
-                scores = contract(key, query, 1, 1) * score_scale + bias[t, set_rows, :]
-                raised = jnp.exp(scores - jnp.max(scores, axis=0, keepdims=True))
-                weights = raised * (1.0 / jnp.sum(raised, axis=0, keepdims=True))
-                weights_low = weights.astype(BF16)
-                att_s[t, :, cols] = contract(weights_low, value, 0, 0).astype(BF16)
-                weight_grad = contract(value, grad, 1, 1)
-                row_term = jnp.sum(weights * weight_grad, axis=0, keepdims=True)
-                score_grad = (weights * (weight_grad - row_term) * score_scale).astype(BF16)
-                qg_s[t, :, cols] = contract(score_grad, key, 0, 0).astype(BF16)
-                for which, (left, right) in enumerate(((score_grad, query), (weights_low, grad))):
+            both = range(2)
+            set_rows = [pl.ds(0, block_rows + plan.far_rows[t]) for t in both]
+            query, grad = [q_s[t, :, cols] for t in both], [cot[t, :, cols] for t in both]
+            key = [keyset[t, 0, set_rows[t], cols] for t in both]
+            value = [keyset[t, 1, set_rows[t], cols] for t in both]
+            scores = [
+                contract(key[t], query[t], 1, 1) * (score_scale / LOG_TWO) + bias[t, set_rows[t], :]
+                for t in both
+            ]
+            weight_grad = [contract(value[t], grad[t], 1, 1) for t in both]
+            raised = [jnp.exp2(part - jnp.max(part, axis=0, keepdims=True)) for part in scores]
+            weights = [part * (1.0 / jnp.sum(part, axis=0, keepdims=True)) for part in raised]
+            weights_low = [part.astype(BF16) for part in weights]
+            row_term = [
+                jnp.sum(weights[t] * weight_grad[t], axis=0, keepdims=True) for t in both
+            ]
+            score_grad = [
+                (weights[t] * ((weight_grad[t] - row_term[t]) * score_scale)).astype(BF16)
+                for t in both
+            ]
+            for t in both:
+                att_s[t, :, cols] = contract(weights_low[t], value[t], 0, 0).astype(BF16)
+                qg_s[t, :, cols] = contract(score_grad[t], key[t], 0, 0).astype(BF16)
+                for which, (left, right) in enumerate(
+                    ((score_grad[t], query[t]), (weights_low[t], grad[t]))
+                ):
                     set_grad = contract(left, right, 1, 0)
                     own[t, which, :, cols] = set_grad[:block_rows]
                     far_grad[t, which, pl.ds(0, plan.far_rows[t]), cols] = set_grad[
@@ -398,30 +434,11 @@
         att_own(group).start()
         result_copy(0, group).start()
         result_own(0, group).start()
-
-    for group in range(GROUPS):
-        for number, (offset, _, _, _) in enumerate(entries):
-
-            @pl.when(inside(pair - offset))
-            def _(group=group, number=number):
-                grad_copy(group, number).wait_recv()
-
-        for u in range(2):
-            _, _, first, rows = plan.uses[1 - u][0]
-            near = pair_matrix(rows, block_rows)
-            returned = pl.ds(0, plan.return_rows[u])
-            for which in range(2):
-                total = own[u, which, :, columns(group)]
-                total = total + contract(
-                    near, far_grad[1 - u, which, pl.ds(first, rows), columns(group)], 0, 0
-                )
-                total = total + contract(
-                    spread[u, returned, :], grecv[u, which, returned, columns(group)], 0, 0
-                )
-                total_s[u, which, :, columns(group)] = total.astype(BF16)
-        for which in (1, 2):
-            result_copy(which, group).start()
-            result_own(which, group).start()
+        if group >= 2:
+            finish(group - 2)
+
+    for group in range(max(0, GROUPS - 2), GROUPS):
+        finish(group)
 
     for group in range(GROUPS):
         att_own(group).wait()

time: 42.9 us -> 39.7 us (0.925)
  Pallas kernels: 42.1 us -> 38.9 us
    pallas_call x1, Pallas kernels: 40.1 us -> 36.9 us  [local(): pl.pallas_call(functools.partial(kernel, plan, heads_axis), out_shape=(ja...]
where the time goes in v5:
time: 39.7 us; the launch traced here: 39.6 us
  Pallas kernels  38.9 us (98%)
  between operations  0.64 us (2%)
    pallas_call x1, Pallas kernels, local(): pl.pallas_call(functools.partial(kernel, plan, heads_axis), out_shape=(ja...  36.9 us
    pallas_call x1, Pallas kernels, local(): pl.pallas_call(write_out, out_shape=tuple((jax.ShapeDtypeStruct(part.shap...  1.98 us

profile of v5, /device:TPU:0, one launch (start us, length us, event | category | flops | bytes accessed | tf_op | source)
XLA Modules:
  0.0 39.6 jit_solution(16322374080020232893)
XLA Ops:
  0.6 36.9 %shard_map.75 = (bf16[32,4096]{1,0:T(8,128)(2,1)}, bf16[128,1024]{1,0:T(8,128)(2,1)}, bf16[128,1024]{1,0:T(8,128)(2,1)}, bf16[128,1024]{1,0:T(8,128)(2,1)}) custom-call(bf16[128,1024]{1,0:T(8,128)(2,1)} %q_hbm.1, bf16[128,1024]{1,0:T(8,128)(2,1)} %k_hbm.1, bf16[128,1024]{1,0:T(8,128)(2,1)} %v_hbm.1, bf16[32,4096]{1,0:T(8,128)(2,1)} %c_hbm.1), custom_call_target="tpu_custom_call" | custom-call | flops 780140544 | bytes 2097152 | tf_op jit(solution)/shard_map/pallas_call | solution.py:525
  37.6 2.0 %shard_map.76 = (bf16[32,4096]{1,0:T(8,128)(2,1)}, bf16[128,1024]{1,0:T(8,128)(2,1)}, bf16[128,1024]{1,0:T(8,128)(2,1)}, bf16[128,1024]{1,0:T(8,128)(2,1)}) custom-call(bf16[32,4096]{1,0:T(8,128)(2,1)} %get-tuple-element.8.refs_0_, bf16[128,1024]{1,0:T(8,128)(2,1)} %get-tuple-element.9.refs_1_, bf16[128,1024]{1,0:T(8,128)(2,1)} %get-tuple-element.10.refs_2_, ...), custom_call_target="tpu_custom_call" | custom-call | tf_op jit(solution)/shard_map/pallas_call | solution.py:540

commit v6 on v5

--- a/solution.py
+++ b/solution.py
@@ -11,6 +11,7 @@
 HEAD_DIM = 128
 LEVELS = 4
 GROUPS = 4
+CHUNK = 2
 
 LOG_TWO = math.log(2.0)
 MASKED = -1e30
@@ -32,13 +33,13 @@
         self.first = []
         self.uses = [[], []]
         self.far_rows = [0, 0]
-        self.returns = [[], []]
-        self.return_rows = [0, 0]
+        self.messages = []
         self.entry_rows = 0
         for t in range(2):
             self.use(t, None, 1, block_rows)
         for distance in range(1, self.reach + 1):
             for offset in (distance, -distance):
+                start = self.entry_rows
                 for part in range(2):
                     gaps = [abs(2 * offset + part - t) for t in range(2)]
                     levels = [gap.bit_length() if gap <= farthest else None for gap in gaps]
@@ -51,21 +52,16 @@
                     self.entries.append((offset, part, level, rows))
                     self.first.append(self.entry_rows)
                     self.entry_rows += rows
-                    self.returns[part].append((number, self.return_rows[part]))
-                    self.return_rows[part] += rows
                     for t in range(2):
                         if levels[t] is not None:
                             self.use(t, number, levels[t], block_rows)
+                self.messages.append((offset, start, self.entry_rows - start))
 
     def use(self, t, number, level, block_rows):
         rows = rows_of(level, block_rows)
         self.uses[t].append((number, level, self.far_rows[t], rows))
         self.far_rows[t] += rows
 
-    def return_first(self, number):
-        part = self.entries[number][1]
-        return dict(self.returns[part])[number]
-
 
 def contract(left, right, left_dim, right_dim):
     return lax.dot_general(
@@ -83,7 +79,7 @@
     plan, heads_axis,
     q_hbm, k_hbm, v_hbm, c_hbm,
     att_out, qg_out, kg_out, vg_out,
-    keyset, q_s, cot, bias, own, far_grad, rbuf, gsend, grecv, spread, att_s, qg_s, total_s, pyramid,
+    keyset, q_s, cot, bias, own, far_grad, rbuf, gsend, grecv, spread, held_s, att_s, qg_s, total_s, pyramid,
     own_sem, cot_own_sem, out_own_sem, att_own_sem, send_in, recv_in, ksend, krecv,
     gsem, gland, csend, crecv, asend, arecv, send_out, recv_out,
 ):
@@ -91,6 +87,8 @@
     out_rows = c_hbm.shape[0]
     half = width // 2
     span = half // GROUPS
+    wide = CHUNK * span
+    chunks = GROUPS // CHUNK
     entries = plan.entries
     position = lax.axis_index("seq")
     my_head = lax.axis_index("head")
@@ -144,46 +142,46 @@
             {"seq": mate, "head": my_head},
         )
 
-    def cot_source(part, other_head, group):
-        first = other_head * width + part * half + group * span
-        return c_hbm.at[:, pl.ds(pl.multiple_of(first, 128), span)]
-
-    def cot_place(group):
-        return cot.at[mine, pl.ds(pl.multiple_of(my_head * out_rows, 16), out_rows), columns(group)]
-
-    def cot_copy(group, step):
+    def cot_source(part, other_head, chunk):
+        first = other_head * width + part * half + chunk * wide
+        return c_hbm.at[:, pl.ds(pl.multiple_of(first, 128), wide)]
+
+    def cot_place(chunk):
+        return cot.at[mine, pl.ds(pl.multiple_of(my_head * out_rows, 16), out_rows), pl.ds(chunk * wide, wide)]
+
+    def cot_copy(chunk, step):
         part, other = seat(step)
         return remote(
-            cot_source(part, other, group), cot_place(group),
-            csend.at[group, step - 1], crecv.at[group, step - 1],
+            cot_source(part, other, chunk), cot_place(chunk),
+            csend.at[chunk, step - 1], crecv.at[chunk, step - 1],
             {"seq": 2 * pair + part, "head": other},
         )
 
-    def cot_own(group):
+    def cot_own(chunk):
         return pltpu.make_async_copy(
-            cot_source(mine, my_head, group), cot_place(group), cot_own_sem.at[group]
-        )
-
-    def att_source(part, other_head, group):
+            cot_source(mine, my_head, chunk), cot_place(chunk), cot_own_sem.at[chunk]
+        )
+
+    def att_source(part, other_head, chunk):
         return att_s.at[
-            part, pl.ds(pl.multiple_of(other_head * out_rows, 16), out_rows), columns(group)
+            part, pl.ds(pl.multiple_of(other_head * out_rows, 16), out_rows), pl.ds(chunk * wide, wide)
         ]
 
-    def att_place(group):
-        first = my_head * width + mine * half + group * span
-        return att_out.at[:, pl.ds(pl.multiple_of(first, 128), span)]
-
-    def att_copy(group, step):
+    def att_place(chunk):
+        first = my_head * width + mine * half + chunk * wide
+        return att_out.at[:, pl.ds(pl.multiple_of(first, 128), wide)]
+
+    def att_copy(chunk, step):
         part, other = seat(step)
         return remote(
-            att_source(part, other, group), att_place(group),
-            asend.at[group, step - 1], arecv.at[group, step - 1],
+            att_source(part, other, chunk), att_place(chunk),
+            asend.at[chunk, step - 1], arecv.at[chunk, step - 1],
             {"seq": 2 * pair + part, "head": other},
         )
 
-    def att_own(group):
+    def att_own(chunk):
         return pltpu.make_async_copy(
-            att_source(mine, my_head, group), att_place(group), att_own_sem.at[group]
+            att_source(mine, my_head, chunk), att_place(chunk), att_own_sem.at[chunk]
         )
 
     def kv_copy(group, number):
@@ -195,10 +193,10 @@
         )
 
     def grad_copy(group, number):
-        offset, part, level, rows = entries[number]
+        offset, first, rows = plan.messages[number]
+        place = (slice(None), pl.ds(first, rows), columns(group))
         return remote(
-            gsend.at[:, pl.ds(plan.first[number], rows), columns(group)],
-            grecv.at[part, :, pl.ds(plan.return_first(number), rows), columns(group)],
+            gsend.at[place], grecv.at[place],
             gsem.at[group, number], gland.at[group, number], rail(pair + offset),
         )
 
@@ -232,14 +230,35 @@
 
     def send_levels(part, group):
         for number, entry in enumerate(entries):
-            if entry[1] == part:
-
-                @pl.when(inside(pair - entry[0]))
-                def _(number=number):
-                    kv_copy(group, number).start()
+
+            @pl.when((part == entry[1]) & inside(pair - entry[0]))
+            def _(number=number):
+                kv_copy(group, number).start()
+
+    def send_near(group):
+        for which in range(2):
+            mate_copy(which, group).start()
+
+    def send_own(group):
+        for which in range(2):
+            own_copy(which, group).wait()
+        make_levels(mine, group)
+        send_levels(mine, group)
+
+    def send_rest(group):
+        mate_copy(2, group).start()
+        if group % CHUNK == 0:
+            for step in range(1, crew):
+                cot_copy(group // CHUNK, step).start()
+
+    def send_mate(group):
+        for which in range(2):
+            mate_copy(which, group).wait_recv()
+        make_levels(1 - mine, group)
+        send_levels(1 - mine, group)
 
     def finish(group):
-        for number, (offset, _, _, _) in enumerate(entries):
+        for number, (offset, _, _) in enumerate(plan.messages):
 
             @pl.when(inside(pair - offset))
             def _(group=group, number=number):
@@ -248,14 +267,13 @@
         for u in range(2):
             _, _, first, rows = plan.uses[1 - u][0]
             near = pair_matrix(rows, block_rows)
-            returned = pl.ds(0, plan.return_rows[u])
             for which in range(2):
                 total = own[u, which, :, columns(group)]
                 total = total + contract(
                     near, far_grad[1 - u, which, pl.ds(first, rows), columns(group)], 0, 0
                 )
                 total = total + contract(
-                    spread[u, returned, :], grecv[u, which, returned, columns(group)], 0, 0
+                    spread[u], grecv[which, :, columns(group)], 0, 0
                 )
                 total_s[u, which, :, columns(group)] = total.astype(BF16)
         for which in (1, 2):
@@ -284,37 +302,17 @@
     for which in range(3):
         for group in range(GROUPS):
             own_copy(which, group).start()
-    for group in range(GROUPS):
-        cot_own(group).start()
+    for chunk in range(chunks):
+        cot_own(chunk).start()
 
     pl.semaphore_wait(barrier, greeted)
-    for group in range(GROUPS):
-        for which in range(2):
-            mate_copy(which, group).start()
-
-    for group in range(GROUPS):
-        for which in range(2):
-            own_copy(which, group).wait()
-        for part in range(2):
-
-            @pl.when(mine == part)
-            def _(part=part, group=group):
-                make_levels(part, group)
-                send_levels(part, group)
-
-    for group in range(GROUPS):
-        for which in range(2):
-            mate_copy(which, group).wait_recv()
-        for part in range(2):
-
-            @pl.when(mine != part)
-            def _(part=part, group=group):
-                make_levels(part, group)
-                send_levels(part, group)
-
-        mate_copy(2, group).start()
-        for step in range(1, crew):
-            cot_copy(group, step).start()
+    send_near(0)
+    send_own(0)
+    send_rest(0)
+    send_near(1)
+    send_own(1)
+    send_mate(0)
+    send_rest(1)
 
     for t in range(2):
         bias[t, own_rows, :] = jnp.zeros((block_rows, block_rows), F32)
@@ -334,24 +332,32 @@
             bias[t, pl.ds(block_rows + first, rows), :] = jnp.where(
                 row < (block_rows >> level), shown, MASKED
             )
-        for number, first in plan.returns[t]:
-            offset, _, level, rows = entries[number]
+        for number, (_, part, level, rows) in enumerate(entries):
             row = lax.broadcasted_iota(jnp.int32, (rows, block_rows), 0)
             col = lax.broadcasted_iota(jnp.int32, (rows, block_rows), 1)
-            spread[t, pl.ds(first, rows), :] = jnp.where(
-                (col >> level) == row, 0.5**level, 0.0
+            taken = (col >> level) == (row if part == t else -1)
+            spread[t, pl.ds(plan.first[number], rows), :] = jnp.where(
+                taken, 0.5**level, 0.0
             ).astype(BF16)
 
-            @pl.when(jnp.logical_not(inside(pair - offset)))
-            def _(t=t, first=first, rows=rows):
-                grecv[t, :, pl.ds(first, rows), :] = jnp.zeros((2, rows, half), BF16)
-
+    for offset, first, rows in plan.messages:
+
+        @pl.when(jnp.logical_not(inside(pair - offset)))
+        def _(first=first, rows=rows):
+            grecv[:, pl.ds(first, rows), :] = jnp.zeros((2, rows, half), BF16)
+
+    send_mate(1)
     for group in range(GROUPS):
+        if group + 2 < GROUPS:
+            send_near(group + 2)
+            send_own(group + 2)
+            send_rest(group + 2)
         own_copy(2, group).wait()
-        cot_own(group).wait()
         mate_copy(2, group).wait_recv()
-        for step in range(1, crew):
-            cot_copy(group, step).wait_recv()
+        if group % CHUNK == 0:
+            cot_own(group // CHUNK).wait()
+            for step in range(1, crew):
+                cot_copy(group // CHUNK, step).wait_recv()
         for t in range(2):
             _, _, first, rows = plan.uses[t][0]
             keyset[t, :, pl.ds(block_rows + first, rows), columns(group)] = pyramid[0][
@@ -374,7 +380,11 @@
                                     t, which, pl.ds(block_rows + first, use_rows), columns(group)
                                 ] = held.astype(BF16)
 
+        if group + 2 < GROUPS:
+            send_mate(group + 2)
+
         def head_pass(head_number, carry, group=group):
+            held = pl.ds(pl.multiple_of(head_number * HEAD_DIM, HEAD_DIM), HEAD_DIM)
             cols = pl.ds(pl.multiple_of(group * span + head_number * HEAD_DIM, HEAD_DIM), HEAD_DIM)
             both = range(2)
             set_rows = [pl.ds(0, block_rows + plan.far_rows[t]) for t in both]
@@ -397,8 +407,8 @@
                 for t in both
             ]
             for t in both:
-                att_s[t, :, cols] = contract(weights_low[t], value[t], 0, 0).astype(BF16)
-                qg_s[t, :, cols] = contract(score_grad[t], key[t], 0, 0).astype(BF16)
+                held_s[t, 0, set_rows[t], held] = score_grad[t]
+                held_s[t, 1, set_rows[t], held] = weights_low[t]
                 for which, (left, right) in enumerate(
                     ((score_grad[t], query[t]), (weights_low[t], grad[t]))
                 ):
@@ -407,6 +417,17 @@
                     far_grad[t, which, pl.ds(0, plan.far_rows[t]), cols] = set_grad[
                         block_rows:
                     ].astype(BF16)
+            return carry
+
+        def token_pass(head_number, carry, group=group):
+            held = pl.ds(pl.multiple_of(head_number * HEAD_DIM, HEAD_DIM), HEAD_DIM)
+            cols = pl.ds(pl.multiple_of(group * span + head_number * HEAD_DIM, HEAD_DIM), HEAD_DIM)
+            for t in range(2):
+                rows = pl.ds(0, block_rows + plan.far_rows[t])
+                for which, out in enumerate((qg_s, att_s)):
+                    out[t, :, cols] = contract(
+                        held_s[t, which, rows, held], keyset[t, which, rows, cols], 0, 0
+                    ).astype(BF16)
             return carry
 
         lax.fori_loop(0, span // HEAD_DIM, head_pass, 0)
@@ -427,37 +448,53 @@
                     gsend[which, pl.ds(plan.first[number], rows), columns(group)] = summed.astype(
                         BF16
                     )
+
+        for number, (offset, _, _) in enumerate(plan.messages):
+
+            @pl.when(inside(pair + offset))
+            def _(group=group, number=number):
                 grad_copy(group, number).start()
 
-        for step in range(1, crew):
-            att_copy(group, step).start()
-        att_own(group).start()
+        lax.fori_loop(0, span // HEAD_DIM, token_pass, 0)
+        if group % CHUNK == CHUNK - 1:
+            for step in range(1, crew):
+                att_copy(group // CHUNK, step).start()
+            att_own(group // CHUNK).start()
         result_copy(0, group).start()
         result_own(0, group).start()
         if group >= 2:
             finish(group - 2)
 
+    for group in range(GROUPS):
+        for which in range(3):
+            mate_copy(which, group).wait_send()
+        for number, (offset, _, _, _) in enumerate(entries):
+
+            @pl.when(inside(pair - offset))
+            def _(group=group, number=number):
+                kv_copy(group, number).wait_send()
+
+    for chunk in range(chunks):
+        for step in range(1, crew):
+            cot_copy(chunk, step).wait_send()
+
     for group in range(max(0, GROUPS - 2), GROUPS):
         finish(group)
 
+    for chunk in range(chunks):
+        att_own(chunk).wait()
+        for step in range(1, crew):
+            att_copy(chunk, step).wait()
     for group in range(GROUPS):
-        att_own(group).wait()
+        for number, (offset, _, _) in enumerate(plan.messages):
+
+            @pl.when(inside(pair + offset))
+            def _(group=group, number=number):
+                grad_copy(group, number).wait_send()
+
         for which in range(3):
             result_own(which, group).wait()
             result_copy(which, group).wait()
-            mate_copy(which, group).wait_send()
-        for step in range(1, crew):
-            cot_copy(group, step).wait_send()
-            att_copy(group, step).wait()
-        for number, (offset, _, _, _) in enumerate(entries):
-
-            @pl.when(inside(pair - offset))
-            def _(group=group, number=number):
-                kv_copy(group, number).wait_send()
-
-            @pl.when(inside(pair + offset))
-            def _(group=group, number=number):
-                grad_copy(group, number).wait_send()
 
 
 def write_out(*refs):
@@ -480,10 +517,12 @@
     plan = Plan(blocks, block_rows)
     half = width // 2
     count = len(plan.entries)
-    far_rows, return_rows = max(plan.far_rows), max(plan.return_rows)
+    far_rows = max(plan.far_rows)
     set_rows = block_rows + far_rows
     levels = max(entry[2] for entry in plan.entries)
     steps = 2 * heads_axis - 1
+    chunks = GROUPS // CHUNK
+    messages = len(plan.messages)
     dma = pltpu.SemaphoreType.DMA
     anywhere = pl.BlockSpec(memory_space=pl.ANY)
     scratch = [
@@ -495,8 +534,9 @@
         pltpu.VMEM((2, 2, far_rows, half), BF16),
         pltpu.VMEM((2, plan.entry_rows, half), BF16),
         pltpu.VMEM((2, plan.entry_rows, half), BF16),
-        pltpu.VMEM((2, 2, return_rows, half), BF16),
-        pltpu.VMEM((2, return_rows, block_rows), BF16),
+        pltpu.VMEM((2, plan.entry_rows, half), BF16),
+        pltpu.VMEM((2, plan.entry_rows, block_rows), BF16),
+        pltpu.VMEM((2, 2, set_rows, half // GROUPS), BF16),
         pltpu.VMEM((2, block_rows, half), BF16),
         pltpu.VMEM((2, block_rows, half), BF16),
         pltpu.VMEM((2, 2, block_rows, half), BF16),
@@ -505,19 +545,19 @@
             for level in range(1, levels + 1)
         ],
         dma((3, GROUPS)),
-        dma((GROUPS,)),
+        dma((chunks,)),
         dma((3, GROUPS)),
-        dma((GROUPS,)),
+        dma((chunks,)),
         dma((3, GROUPS)),
         dma((3, GROUPS)),
         dma((GROUPS, count)),
         dma((GROUPS, count)),
-        dma((GROUPS, count)),
-        dma((GROUPS, count)),
-        dma((GROUPS, steps)),
-        dma((GROUPS, steps)),
-        dma((GROUPS, steps)),
-        dma((GROUPS, steps)),
+        dma((GROUPS, messages)),
+        dma((GROUPS, messages)),
+        dma((chunks, steps)),
+        dma((chunks, steps)),
+        dma((chunks, steps)),
+        dma((chunks, steps)),
         dma((3, GROUPS)),
         dma((3, GROUPS)),
     ]

time: 39.7 us -> 43.6 us (1.098)
  Pallas kernels: 38.9 us -> 42.8 us
    pallas_call x1, Pallas kernels: 36.9 us -> 40.8 us  [local(): pl.pallas_call(functools.partial(kernel, plan, heads_axis), out_shape=(ja...]
where the time goes in v6:
time: 43.6 us; the launch traced here: 43.4 us
  Pallas kernels  42.8 us (98%)
  between operations  0.64 us (1%)
    pallas_call x1, Pallas kernels, local(): pl.pallas_call(functools.partial(kernel, plan, heads_axis), out_shape=(ja...  40.8 us
    pallas_call x1, Pallas kernels, local(): pl.pallas_call(write_out, out_shape=tuple((jax.ShapeDtypeStruct(part.shap...  1.98 us

profile of v6, /device:TPU:0, one launch (start us, length us, event | category | flops | bytes accessed | tf_op | source)
XLA Modules:
  0.0 43.4 jit_solution(3639414022921234670)
XLA Ops:
  0.6 40.8 %shard_map.75 = (bf16[32,4096]{1,0:T(8,128)(2,1)}, bf16[128,1024]{1,0:T(8,128)(2,1)}, bf16[128,1024]{1,0:T(8,128)(2,1)}, bf16[128,1024]{1,0:T(8,128)(2,1)}) custom-call(bf16[128,1024]{1,0:T(8,128)(2,1)} %q_hbm.1, bf16[128,1024]{1,0:T(8,128)(2,1)} %k_hbm.1, bf16[128,1024]{1,0:T(8,128)(2,1)} %v_hbm.1, bf16[32,4096]{1,0:T(8,128)(2,1)} %c_hbm.1), custom_call_target="tpu_custom_call" | custom-call | flops 780140544 | bytes 2097152 | tf_op jit(solution)/shard_map/pallas_call | solution.py:565
  41.4 2.0 %shard_map.76 = (bf16[32,4096]{1,0:T(8,128)(2,1)}, bf16[128,1024]{1,0:T(8,128)(2,1)}, bf16[128,1024]{1,0:T(8,128)(2,1)}, bf16[128,1024]{1,0:T(8,128)(2,1)}) custom-call(bf16[32,4096]{1,0:T(8,128)(2,1)} %get-tuple-element.8.refs_0_, bf16[128,1024]{1,0:T(8,128)(2,1)} %get-tuple-element.9.refs_1_, bf16[128,1024]{1,0:T(8,128)(2,1)} %get-tuple-element.10.refs_2_, ...), custom_call_target="tpu_custom_call" | custom-call | tf_op jit(solution)/shard_map/pallas_call | solution.py:580

commit v7 on v6

--- a/solution.py
+++ b/solution.py
@@ -11,7 +11,7 @@
 HEAD_DIM = 128
 LEVELS = 4
 GROUPS = 4
-CHUNK = 2
+CHUNK = 1
 
 LOG_TWO = math.log(2.0)
 MASKED = -1e30
@@ -79,7 +79,7 @@
     plan, heads_axis,
     q_hbm, k_hbm, v_hbm, c_hbm,
     att_out, qg_out, kg_out, vg_out,
-    keyset, q_s, cot, bias, own, far_grad, rbuf, gsend, grecv, spread, held_s, att_s, qg_s, total_s, pyramid,
+    keyset, q_s, cot, bias, own, far_grad, rbuf, gsend, grecv, spread, att_s, qg_s, total_s, pyramid,
     own_sem, cot_own_sem, out_own_sem, att_own_sem, send_in, recv_in, ksend, krecv,
     gsem, gland, csend, crecv, asend, arecv, send_out, recv_out,
 ):
@@ -306,13 +306,15 @@
         cot_own(chunk).start()
 
     pl.semaphore_wait(barrier, greeted)
-    send_near(0)
-    send_own(0)
-    send_rest(0)
-    send_near(1)
-    send_own(1)
-    send_mate(0)
-    send_rest(1)
+    for group in range(GROUPS):
+        send_near(group)
+        send_rest(group)
+        if group == 0:
+            send_own(0)
+    for group in range(1, GROUPS):
+        send_own(group)
+        if group == 1:
+            send_mate(0)
 
     for t in range(2):
         bias[t, own_rows, :] = jnp.zeros((block_rows, block_rows), F32)
@@ -348,10 +350,6 @@
 
     send_mate(1)
     for group in range(GROUPS):
-        if group + 2 < GROUPS:
-            send_near(group + 2)
-            send_own(group + 2)
-            send_rest(group + 2)
         own_copy(2, group).wait()
         mate_copy(2, group).wait_recv()
         if group % CHUNK == 0:
@@ -384,7 +382,6 @@
             send_mate(group + 2)
 
         def head_pass(head_number, carry, group=group):
-            held = pl.ds(pl.multiple_of(head_number * HEAD_DIM, HEAD_DIM), HEAD_DIM)
             cols = pl.ds(pl.multiple_of(group * span + head_number * HEAD_DIM, HEAD_DIM), HEAD_DIM)
             both = range(2)
             set_rows = [pl.ds(0, block_rows + plan.far_rows[t]) for t in both]
@@ -407,8 +404,8 @@
                 for t in both
             ]
             for t in both:
-                held_s[t, 0, set_rows[t], held] = score_grad[t]
-                held_s[t, 1, set_rows[t], held] = weights_low[t]
+                att_s[t, :, cols] = contract(weights_low[t], value[t], 0, 0).astype(BF16)
+                qg_s[t, :, cols] = contract(score_grad[t], key[t], 0, 0).astype(BF16)
                 for which, (left, right) in enumerate(
                     ((score_grad[t], query[t]), (weights_low[t], grad[t]))
                 ):
@@ -417,17 +414,6 @@
                     far_grad[t, which, pl.ds(0, plan.far_rows[t]), cols] = set_grad[
                         block_rows:
                     ].astype(BF16)
-            return carry
-
-        def token_pass(head_number, carry, group=group):
-            held = pl.ds(pl.multiple_of(head_number * HEAD_DIM, HEAD_DIM), HEAD_DIM)
-            cols = pl.ds(pl.multiple_of(group * span + head_number * HEAD_DIM, HEAD_DIM), HEAD_DIM)
-            for t in range(2):
-                rows = pl.ds(0, block_rows + plan.far_rows[t])
-                for which, out in enumerate((qg_s, att_s)):
-                    out[t, :, cols] = contract(
-                        held_s[t, which, rows, held], keyset[t, which, rows, cols], 0, 0
-                    ).astype(BF16)
             return carry
 
         lax.fori_loop(0, span // HEAD_DIM, head_pass, 0)
@@ -455,7 +441,6 @@
             def _(group=group, number=number):
                 grad_copy(group, number).start()
 
-        lax.fori_loop(0, span // HEAD_DIM, token_pass, 0)
         if group % CHUNK == CHUNK - 1:
             for step in range(1, crew):
                 att_copy(group // CHUNK, step).start()
@@ -536,7 +521,6 @@
         pltpu.VMEM((2, plan.entry_rows, half), BF16),
         pltpu.VMEM((2, plan.entry_rows, half), BF16),
         pltpu.VMEM((2, plan.entry_rows, block_rows), BF16),
-        pltpu.VMEM((2, 2, set_rows, half // GROUPS), BF16),
         pltpu.VMEM((2, block_rows, half), BF16),
         pltpu.VMEM((2, block_rows, half), BF16),
         pltpu.VMEM((2, 2, block_rows, half), BF16),

time: 43.6 us -> 40.9 us (0.938)
  Pallas kernels: 42.8 us -> 40.1 us
    pallas_call x1, Pallas kernels: 40.8 us -> 38.1 us  [local(): pl.pallas_call(functools.partial(kernel, plan, heads_axis), out_shape=(ja...]
where the time goes in v7:
time: 40.9 us; the launch traced here: 40.7 us
  Pallas kernels  40.1 us (98%)
  between operations  0.64 us (2%)
    pallas_call x1, Pallas kernels, local(): pl.pallas_call(functools.partial(kernel, plan, heads_axis), out_shape=(ja...  38.1 us
    pallas_call x1, Pallas kernels, local(): pl.pallas_call(write_out, out_shape=tuple((jax.ShapeDtypeStruct(part.shap...  1.98 us

profile of v7, /device:TPU:0, one launch (start us, length us, event | category | flops | bytes accessed | tf_op | source)
XLA Modules:
  0.0 40.7 jit_solution(159404968470069295)
XLA Ops:
  0.6 38.1 %shard_map.75 = (bf16[32,4096]{1,0:T(8,128)(2,1)}, bf16[128,1024]{1,0:T(8,128)(2,1)}, bf16[128,1024]{1,0:T(8,128)(2,1)}, bf16[128,1024]{1,0:T(8,128)(2,1)}) custom-call(bf16[128,1024]{1,0:T(8,128)(2,1)} %q_hbm.1, bf16[128,1024]{1,0:T(8,128)(2,1)} %k_hbm.1, bf16[128,1024]{1,0:T(8,128)(2,1)} %v_hbm.1, bf16[32,4096]{1,0:T(8,128)(2,1)} %c_hbm.1), custom_call_target="tpu_custom_call" | custom-call | flops 780140544 | bytes 2097152 | tf_op jit(solution)/shard_map/pallas_call | solution.py:549
  38.7 2.0 %shard_map.76 = (bf16[32,4096]{1,0:T(8,128)(2,1)}, bf16[128,1024]{1,0:T(8,128)(2,1)}, bf16[128,1024]{1,0:T(8,128)(2,1)}, bf16[128,1024]{1,0:T(8,128)(2,1)}) custom-call(bf16[32,4096]{1,0:T(8,128)(2,1)} %get-tuple-element.8.refs_0_, bf16[128,1024]{1,0:T(8,128)(2,1)} %get-tuple-element.9.refs_1_, bf16[128,1024]{1,0:T(8,128)(2,1)} %get-tuple-element.10.refs_2_, ...), custom_call_target="tpu_custom_call" | custom-call | tf_op jit(solution)/shard_map/pallas_call | solution.py:564
